TPU v7x, 512 devices: a whole 4x4x16 slice. The times are simulated.
512 devices in a mesh: lon: 128 (over z, x, y_lo), lev: 4 (over y_hi, core).
Axes of the slice: x: 4, y: 4 (y_hi: 2, y_lo: 2; y = y_hi * 2 + y_lo), z: 16, core: 2. Of those that a mesh axis runs over, the one named last changes fastest.
Arguments:
- fields: bfloat16 [16, 8, 2048, 384], P('lev', None, 'lon'), may hold values from -6 to 6
- counts: int32 [8], replicated, may hold values from 2033 to 2048, as said below
- shifts: int32 [2], replicated, may hold values from 0 to 15, as said below
- norm_gains: float32 [3, 384], replicated, may hold values from 0.5 to 1.5
- window_qkv: bfloat16 [3, 384, 384], replicated
- window_out: bfloat16 [384, 384], replicated, may hold values from -0.3125 to 0.3125
- column_qkv: bfloat16 [3, 384, 384], replicated
- column_out: bfloat16 [384, 384], replicated, may hold values from -0.3125 to 0.3125
- mlp_in: bfloat16 [384, 768], replicated, may hold values from -0.3125 to 0.3125
- mlp_out: bfloat16 [768, 384], replicated, may hold values from -0.21875 to 0.21875
Outputs:
- block_out: bfloat16 [16, 8, 2048, 384], P('lev', None, 'lon')
Inputs may be any that keep to these rules, and one draw needn't show every extreme that they name: Cells 0 to counts[r] - 1 of row r are real, the others padding; some row has all 2048 real and some row exactly 2033. `shifts`: some block of rows has the offset 16 - 1.
All inputs are finite; a program needn't handle non-finite values.
Results may differ from a plain program's by a relative error of at most 0.015.
Values may be sent and summed in bfloat16 or wider, within the bound.
No kernel may reach another device: no remote copies, remote signals or barrier semaphores. Data moves between devices by JAX's collectives and lax.ppermute only.
A program may use at most 64 MiB of HBM per device.

v0:
```python
import math

import jax
import jax.numpy as jnp
from jax import lax
from jax.sharding import PartitionSpec as P

HEADS = 12
WIN_ROWS = 4
WIN_LON = 16


EPSILON = 1e-05


def from_behind(value, axis, steps):
    count = lax.axis_size(axis)
    pairs = [(source, (source + steps) % count) for source in range(count)]
    return lax.ppermute(value, axis, pairs)


def layer_norm(values, gain_row):
    values = values.astype(jnp.float32)
    average = jnp.mean(values, axis=-1, keepdims=True)
    centred = values - average
    variance = jnp.mean(centred * centred, axis=-1, keepdims=True)
    return (centred * lax.rsqrt(variance + EPSILON) * gain_row).astype(jnp.bfloat16)


def softmax_rows(scores):
    highest = jnp.max(scores, axis=-1, keepdims=True)
    weights = jnp.exp(scores - highest)
    return (weights / jnp.sum(weights, axis=-1, keepdims=True)).astype(jnp.bfloat16)


def project_three(normed, weights):
    return jnp.einsum("tw,iwv->itv", normed, weights, preferred_element_type=jnp.float32).astype(
        jnp.bfloat16
    )


def window_attend(queries, keys_in, values_in, key_valid):
    level_count, row_count, cell_count, model_width = queries.shape
    head_size = model_width // HEADS
    windows = cell_count // WIN_LON

    def to_windows(tensor):
        tensor = tensor.reshape(level_count, row_count, windows, WIN_LON, HEADS, head_size)
        tensor = tensor.transpose(0, 2, 4, 1, 3, 5)
        return tensor.reshape(level_count, windows, HEADS, row_count * WIN_LON, head_size)

    scores = jnp.einsum(
        "lnhqd,lnhkd->lnhqk",
        to_windows(queries),
        to_windows(keys_in),
        preferred_element_type=jnp.float32,
    ) / math.sqrt(head_size)
    allowed = (
        key_valid.reshape(row_count, windows, WIN_LON)
        .transpose(1, 0, 2)
        .reshape(windows, row_count * WIN_LON)
    )
    scores = jnp.where(allowed[None, :, None, None, :], scores, -jnp.inf)
    weights_bf = softmax_rows(scores)
    combined = jnp.einsum(
        "lnhqk,lnhkd->lnhqd", weights_bf, to_windows(values_in), preferred_element_type=jnp.float32
    ).astype(jnp.bfloat16)
    combined = combined.reshape(
        level_count, windows, HEADS, row_count, WIN_LON, head_size
    ).transpose(0, 3, 1, 4, 2, 5)
    return combined.reshape(level_count, row_count, cell_count, model_width)


def column_finish(resident, queries, keys_in, values_in, norm_gains, column_out, mlp_in, mlp_out):
    query_levels, columns, model_width = queries.shape
    head_size = model_width // HEADS
    split_q = queries.reshape(query_levels, columns, HEADS, head_size)
    split_k = keys_in.reshape(keys_in.shape[0], columns, HEADS, head_size)
    split_v = values_in.reshape(values_in.shape[0], columns, HEADS, head_size)
    scores = jnp.einsum(
        "qnhd,knhd->nhqk", split_q, split_k, preferred_element_type=jnp.float32
    ) / math.sqrt(head_size)
    weights_bf = softmax_rows(scores)
    combined = jnp.einsum(
        "nhqk,knhd->qnhd", weights_bf, split_v, preferred_element_type=jnp.float32
    ).astype(jnp.bfloat16)
    combined = combined.reshape(-1, model_width)
    updated = resident.reshape(-1, model_width).astype(jnp.float32) + jnp.dot(
        combined, column_out, preferred_element_type=jnp.float32
    )
    updated = updated.astype(jnp.bfloat16)
    normed = layer_norm(updated, norm_gains[2])
    inner_act = jax.nn.gelu(jnp.dot(normed, mlp_in, preferred_element_type=jnp.float32)).astype(
        jnp.bfloat16
    )
    result = updated.astype(jnp.float32) + jnp.dot(
        inner_act, mlp_out, preferred_element_type=jnp.float32
    )
    return result.astype(jnp.bfloat16).reshape(query_levels, columns, model_width)


def forward_windows(extended, counts, shifts, anchor, circle, cell_count):
    row_count = extended.shape[2]
    row_blocks = row_count // WIN_ROWS
    regions = []
    for row_block in range(row_blocks):
        offset = shifts[row_block]
        first_row = row_block * WIN_ROWS
        region = lax.dynamic_slice_in_dim(
            extended[:, :, first_row : first_row + WIN_ROWS], offset, cell_count, 3
        )
        places = (anchor + offset + jnp.arange(cell_count, dtype=jnp.int32)) % circle
        key_valid = places[None, :] < counts[first_row : first_row + WIN_ROWS, None]
        regions.append(window_attend(region[0], region[1], region[2], key_valid))
    whole_region = jnp.concatenate(regions, axis=1)
    behind = from_behind(whole_region, "lon", 1)
    joined = jnp.concatenate([behind, whole_region], axis=2)
    pieces = []
    for row_block in range(row_blocks):
        offset = shifts[row_block]
        first_row = row_block * WIN_ROWS
        pieces.append(
            lax.dynamic_slice_in_dim(
                joined[:, first_row : first_row + WIN_ROWS], WIN_LON - offset, cell_count, 2
            )
        )
    return pieces


def local(
    fields,
    counts,
    shifts,
    norm_gains,
    window_qkv,
    window_out,
    column_qkv,
    column_out,
    mlp_in,
    mlp_out,
):
    level_count, row_count, cell_count, model_width = fields.shape
    circle = cell_count * lax.axis_size("lon")
    anchor = lax.axis_index("lon") * cell_count
    pieces = []
    normed = layer_norm(fields, norm_gains[0]).reshape(-1, model_width)
    triple = project_three(normed, window_qkv).reshape(
        3, level_count, row_count, cell_count, model_width
    )
    ahead_cells = from_behind(triple, "lon", -1)
    extended = jnp.concatenate([triple, ahead_cells], axis=3)
    pieces = forward_windows(extended, counts, shifts, anchor, circle, cell_count)
    attended = jnp.concatenate(pieces, axis=1).reshape(-1, model_width)
    resident = fields.reshape(-1, model_width).astype(jnp.float32) + jnp.dot(
        attended, window_out, preferred_element_type=jnp.float32
    )
    resident = resident.astype(jnp.bfloat16).reshape(fields.shape)
    column_piece = lax.all_to_all(resident, "lev", split_axis=2, concat_axis=0, tiled=True)
    full_levels = column_piece.shape[0]
    flat_piece = layer_norm(column_piece, norm_gains[1]).reshape(-1, model_width)
    col_triple = project_three(flat_piece, column_qkv).reshape(3, full_levels, -1, model_width)
    finished = column_finish(
        column_piece.reshape(full_levels, -1, model_width),
        col_triple[0],
        col_triple[1],
        col_triple[2],
        norm_gains,
        column_out,
        mlp_in,
        mlp_out,
    )
    finished = finished.reshape(column_piece.shape)
    layer_out = lax.all_to_all(finished, "lev", split_axis=0, concat_axis=2, tiled=True)
    places = anchor + jnp.arange(cell_count, dtype=jnp.int32)
    live_cells = places[None, :] < counts[:, None]
    return jnp.where(live_cells[None, :, :, None], layer_out, jnp.zeros((), jnp.bfloat16))


def solution(mesh):
    return jax.shard_map(
        local,
        mesh=mesh,
        in_specs=(P("lev", None, "lon", None), P(), P(), P(), P(), P(), P(), P(), P(), P()),
        out_specs=P("lev", None, "lon", None),
        check_vma=False,
    )
```

profile of v0, /device:TPU:1, one launch (start us, length us, event | category | flops | bytes accessed | tf_op | source)
XLA Modules:
  0.0 152.1 jit_solution(738633358092900360)
XLA Ops:
  0.0 0.8 slice_reduce_fusion
  0.8 1.1 convert_reduce_fusion
  2.0 1.3 multiply_reduce_fusion.3
  3.3 1.2 multiply_convert_fusion.2
  4.5 0.8 convolution_convert_fusion.2
  5.3 15.2 %collective-permute-start = (bf16[3,4,8,16,384]{4,3,2,1,0:T(8,128)(2,1)S(1)}, bf16[3,4,8,16,384]{4,3,2,1,0:T(8,128)(2,1)S(1)}, u32[]{:S(2)}, u32[]{:S(2)}) collective-permute-start(bf16[3,4,8,16,384]{4,3,2,1,0:T(8,128)(2,1)S(1)} %bitcast.92), channel_id=1, source_target_pairs={{0,508},{4,0},{8,4},{12,8},{16,12},{20,16},{24,20},{28,24},{32,28}... | collective-permute-start | bytes 3538952 | tf_op jit(solution)/shard_map/ppermute | solution.py:19
  20.5 0.6 fusion.78
  25.1 0.1 lt.92
  25.2 0.1 lt.86
  26.6 1.2 pad_slice_fusion.1
  27.8 17.3 %collective-permute-done = bf16[3,4,8,16,384]{4,3,2,1,0:T(8,128)(2,1)S(1)} collective-permute-done((bf16[3,4,8,16,384]{4,3,2,1,0:T(8,128)(2,1)S(1)}, bf16[3,4,8,16,384]{4,3,2,1,0:T(8,128)(2,1)S(1)}, u32[]{:S(2)}, u32[]{:S(2)}) %collective-permute-start) | collective-permute-done | bytes 1179680 | tf_op jit(solution)/shard_map/ppermute | solution.py:19
  45.1 0.5 fusion.42
  45.6 0.7 fusion.75
  46.3 1.8 %reshape_squeeze.30 = bf16[4,4,1,16,12,32]{5,4,3,1,0,2:T(8,128)(2,1)S(1)} reshape(bf16[1,4,4,16,384]{4,3,2,1,0:T(8,128)(2,1)} %get-tuple-element.11) | data formatting | bytes 393216 | tf_op jit(solution)/shard_map/reshape;squeeze | solution.py:48
  48.1 1.8 %reshape_squeeze.31 = bf16[4,4,1,16,12,32]{5,4,3,1,0,2:T(8,128)(2,1)} reshape(bf16[1,4,4,16,384]{4,3,2,1,0:T(8,128)(2,1)S(1)} %get-tuple-element.12) | data formatting | bytes 393216 | tf_op jit(solution)/shard_map/reshape;squeeze | solution.py:48
  49.9 2.9 %multiply_select_fusion = f32[4,12,64,64]{2,3,1,0:T(8,128)} fusion(bf16[4,12,64,32]{3,1,2,0:T(8,128)(2,1)} %bitcast.108, bf16[4,12,64,32]{3,1,2,0:T(8,128)(2,1)S(1)} %bitcast.104, pred[64]{0:T(512)(128)(4,1)S(1)} %lt.92), kind=kOutput, calls=%fused_computation.28 | convolution fusion | flops 12976128 | bytes 1179712 | tf_op jit(solution)/shard_map/lnhqd,lnhkd->lnhqk/dot_general | solution.py:52
  52.8 2.7 %fusion.84 = f32[4,12,64]{2,1,0:T(8,128)} fusion(bf16[4,12,64,32]{3,1,2,0:T(8,128)(2,1)} %bitcast.109, bf16[4,12,64,32]{3,1,2,0:T(8,128)(2,1)S(1)} %bitcast.105, pred[64]{0:T(512)(128)(4,1)S(1)} %lt.92), kind=kOutput, calls=%fused_computation.121 | convolution fusion | flops 13369407 | bytes 405568 | tf_op jit(solution)/shard_map/sub | solution.py:32
  55.5 0.1 pad_slice_fusion
  55.7 1.1 copy-done.2
  56.8 0.5 dynamic-slice_maximum_fusion
  57.2 0.7 fusion.76
  58.0 0.8 reshape_squeeze.28
  58.8 2.0 %reshape_squeeze.27 = bf16[4,4,1,16,12,32]{5,4,3,1,0,2:T(8,128)(2,1)S(1)} reshape(bf16[1,4,4,16,384]{4,3,2,1,0:T(8,128)(2,1)} %get-tuple-element.14) | data formatting | bytes 393216 | tf_op jit(solution)/shard_map/reshape;squeeze | solution.py:48
  60.8 1.7 %multiply_select_fusion.1 = f32[4,12,64,64]{2,3,1,0:T(8,128)} fusion(bf16[4,12,64,32]{3,1,2,0:T(8,128)(2,1)S(1)} %bitcast.106, bf16[4,12,64,32]{3,1,2,0:T(8,128)(2,1)S(1)} %bitcast.110, pred[64]{0:T(512)(128)(4,1)S(1)} %lt.86), kind=kOutput, calls=%fused_computation.30 | convolution fusion | flops 12976128 | bytes 1179712 | tf_op jit(solution)/shard_map/lnhqd,lnhkd->lnhqk/dot_general | solution.py:52
  62.5 0.9 fusion.79
  63.3 0.8 reshape_squeeze.32
  64.1 2.5 %convolution_convert_fusion.3 = bf16[4,12,64,32]{2,3,1,0:T(8,128)(2,1)S(1)} fusion(bf16[4,12,64,32]{3,1,2,0:T(8,128)(2,1)S(1)} %bitcast.112, f32[4,12,64]{2,1,0:T(8,128)S(1)} %copy-done.9, f32[4,12,64,64]{2,3,1,0:T(8,128)} %multiply_select_fusion), kind=kOutput, calls=%fused_computation.44 | convolution fusion | flops 13274175 | bytes 1191936 | tf_op jit(solution)/shard_map/lnhqk,lnhkd->lnhqd/dot_general | solution.py:65
  66.6 0.8 copy.136
  67.4 0.7 reshape.290
  68.1 0.8 reshape_squeeze.29
  68.9 2.5 %convolution_convert_fusion.4 = bf16[4,12,64,32]{2,3,1,0:T(8,128)(2,1)S(1)} fusion(bf16[4,12,64,32]{3,1,2,0:T(8,128)(2,1)S(1)} %bitcast.113, f32[4,12,64]{2,1,0:T(8,128)S(1)} %fusion.79, f32[4,12,64,64]{2,3,1,0:T(8,128)} %multiply_select_fusion.1), kind=kOutput, calls=%fused_computation.45 | convolution fusion | flops 13274175 | bytes 1191936 | tf_op jit(solution)/shard_map/lnhqk,lnhkd->lnhqd/dot_general | solution.py:65
  71.4 0.8 copy.126
  72.2 0.7 reshape.285
  72.9 1.9 %collective-permute-start.1 = (bf16[4,8,16,384]{3,2,1,0:T(8,128)(2,1)S(1)}, bf16[4,8,16,384]{3,2,1,0:T(8,128)(2,1)S(1)}, u32[]{:S(2)}, u32[]{:S(2)}) collective-permute-start(bf16[4,8,16,384]{3,2,1,0:T(8,128)(2,1)S(1)} %constant_dynamic-update-slice_fusion), channel_id=1, source_target_pairs={{0,4},{4,8},{8,12},{12,16},{16,20},{20,24},{24,28},{28,32},{32,36}... | collective-permute-start | bytes 1179656 | tf_op jit(solution)/shard_map/ppermute | solution.py:19
  77.5 11.7 %collective-permute-done.1 = bf16[4,8,16,384]{3,2,1,0:T(8,128)(2,1)S(1)} collective-permute-done((bf16[4,8,16,384]{3,2,1,0:T(8,128)(2,1)S(1)}, bf16[4,8,16,384]{3,2,1,0:T(8,128)(2,1)S(1)}, u32[]{:S(2)}, u32[]{:S(2)}) %collective-permute-start.1) | collective-permute-done | bytes 393248 | tf_op jit(solution)/shard_map/ppermute | solution.py:19
  89.2 0.1 dynamic-slice_maximum_fusion.1
  89.3 0.2 fusion.55
  89.6 0.4 fusion.29
  90.0 14.1 %all_to_all.27 = bf16[4,8,16,384]{3,1,0,2:T(8,128)(2,1)S(1)} all-to-all(bf16[4,8,16,384]{3,1,0,2:T(8,128)(2,1)S(1)} %copy.97), channel_id=1, replica_groups=mesh['lon'=128,'lev'=4] {'lev'}, dimensions={2} | all-to-all | bytes 786432 | tf_op jit(solution)/shard_map/all_to_all | solution.py:158
  104.2 0.6 fusion.73
  104.8 0.5 copy.185
  105.3 0.8 multiply_reduce_fusion.2
  106.1 0.1 div.67
  106.3 0.1 rsqrt.29
  106.4 0.3 reshape.295
  106.7 0.9 fusion.27
  107.6 0.1 fusion.74
  107.7 2.6 %reshape.301 = bf16[16,32,12,32]{3,2,1,0:T(8,128)(2,1)} reshape(bf16[1,512,384]{2,1,0:T(8,128)(2,1)S(1)} %get-tuple-element.10) | data formatting | bytes 786432 | tf_op jit(solution)/shard_map/reshape;squeeze | solution.py:77
  110.2 2.6 %reshape.302 = bf16[16,32,12,32]{3,2,1,0:T(8,128)(2,1)} reshape(bf16[1,512,384]{2,1,0:T(8,128)(2,1)S(1)} %get-tuple-element.9) | data formatting | bytes 786432 | tf_op jit(solution)/shard_map/reshape;squeeze | solution.py:78
  112.8 4.1 %fusion.16 = f32[32,12,16,16]{2,3,1,0:T(8,128)S(1)} fusion(bf16[16,32,12,32]{3,2,1,0:T(8,128)(2,1)} %reshape.302, bf16[16,32,12,32]{3,2,1,0:T(8,128)(2,1)} %reshape.301), kind=kOutput, calls=%fused_computation.21 | convolution fusion | flops 6291456 | bytes 1179648 | tf_op jit(solution)/shard_map/qnhd,knhd->nhqk/dot_general | solution.py:80
  117.0 2.8 %fusion.89 = (f32[32,12,16]{2,1,0:T(8,128)S(1)}, f32[32,12,16,16]{2,3,1,0:T(8,128)}) fusion(f32[32,12,16,16]{2,3,1,0:T(8,128)S(1)} %fusion.16), kind=kOutput, calls=%fused_computation.122 | output fusion | flops 393231 | bytes 811008 | tf_op jit(solution)/shard_map/sub | solution.py:32
  119.8 2.5 %reshape.300 = bf16[16,32,12,32]{3,2,1,0:T(8,128)(2,1)} reshape(bf16[1,512,384]{2,1,0:T(8,128)(2,1)S(1)} %get-tuple-element.8) | data formatting | bytes 786432 | tf_op jit(solution)/shard_map/reshape;squeeze | solution.py:79
  122.3 5.0 %fusion.22 = bf16[16,32,12,32]{3,0,2,1:T(8,128)(2,1)} fusion(f32[32,12,16,16]{2,3,1,0:T(8,128)} %get-tuple-element.22, f32[32,12,16]{2,1,0:T(8,128)S(1)} %get-tuple-element.21, bf16[16,32,12,32]{3,2,1,0:T(8,128)(2,1)} %reshape.300), kind=kOutput, calls=%fused_computation.33 | convolution fusion | flops 6684672 | bytes 1204224 | tf_op jit(solution)/shard_map/nhqk,knhd->qnhd/dot_general | solution.py:84
  127.3 3.9 %copy.106 = bf16[16,32,12,32]{1,0,3,2:T(8,128)(2,1)S(1)} copy(bf16[16,32,12,32]{3,0,2,1:T(8,128)(2,1)} %fusion.22) | data formatting | bytes 786432 | tf_op jit(solution)/shard_map/convert_element_type | solution.py:86
  131.3 2.3 %reshape.293 = bf16[512,384]{0,1:T(8,128)(2,1)} reshape(bf16[16,32,12,32]{1,0,3,2:T(8,128)(2,1)S(1)} %copy.106) | data formatting | bytes 786432 | tf_op jit(solution)/shard_map/reshape | solution.py:87
  133.5 1.6 %fusion.90 = (f32[512]{0:T(512)S(1)}, f32[512,384]{1,0:T(8,128)S(1)}) fusion(f32[512,384]{1,0:T(8,128)S(1)} %reshape.295, bf16[512,384]{0,1:T(8,128)(2,1)} %reshape.293, bf16[384,384]{1,0:T(8,128)(2,1)S(1)} %copy-done.4), kind=kOutput, calls=%fused_computation.123 | convolution fusion | flops 151780864 | bytes 2263040 | tf_op jit(solution)/shard_map/dot_general | solution.py:88
  135.1 0.2 multiply_reduce_fusion.1
  135.4 2.2 %fusion.28 = bf16[512,384]{1,0:T(8,128)(2,1)S(1)} fusion(f32[512,384]{1,0:T(8,128)S(1)} %get-tuple-element.24, bf16[768,384]{1,0:T(8,128)(2,1)S(1)} %copy-done.8, bf16[384,768]{1,0:T(8,128)(2,1)} %param.18, f32[384]{0:T(512)S(1)} %get-tuple-element.5, f32[512]{0:T(512)S(1)} %add_rsqrt_fusion.2, f32[512]{0:T(512)S(1)} %broadcast_multiply_fusion.2), kind=kOutput, calls=%fused_computation.40 | convolution fusion | flops 608698368 | bytes 2364928 | tf_op jit(solution)/shard_map/dot_general | solution.py:96
  137.6 0.8 reshape_reshape.4
  138.5 4.5 %all-to-all-start.1 = ((bf16[16,8,4,384]{3,2,1,0:T(4,128)(2,1)}), bf16[16,8,4,384]{3,2,1,0:T(4,128)(2,1)S(1)}, u32[]{:S(2)}, u32[]{:S(2)}) async-start(bf16[16,8,4,384]{3,2,1,0:T(4,128)(2,1)} %reshape_reshape.4), calls=%async_computation.1 | async-start | bytes 786432 | tf_op jit(solution)/shard_map/all_to_all | solution.py:173
  143.0 8.0 %all-to-all-done.1 = bf16[16,8,4,384]{3,2,1,0:T(4,128)(2,1)S(1)} async-done(((bf16[16,8,4,384]{3,2,1,0:T(4,128)(2,1)}), bf16[16,8,4,384]{3,2,1,0:T(4,128)(2,1)S(1)}, u32[]{:S(2)}, u32[]{:S(2)}) %all-to-all-start.1) | async-done | bytes 393248 | tf_op jit(solution)/shard_map/all_to_all | solution.py:173
  151.0 0.1 copy.186
  151.2 0.1 all_to_all.24
  151.3 0.9 broadcast_select_fusion
  (38 shorter events, 0.7 us)
Async XLA Ops:
  0.0 4.5 %copy-start = (bf16[3,384,384]{2,1,0:T(8,128)(2,1)S(1)}, bf16[3,384,384]{2,1,0:T(8,128)(2,1)}, u32[]{:S(2)}) copy-start(bf16[3,384,384]{2,1,0:T(8,128)(2,1)} %param.14) | copy-start | bytes 2654212
  3.3 17.2 %copy-start.7 = (s32[2]{0:T(128)S(1)}, s32[2]{0:T(128)}, u32[]{:S(2)}) copy-start(s32[2]{0:T(128)} %param.12) | copy-start | bytes 28
  3.3 21.6 %copy-start.6 = (s32[8]{0:T(128)S(1)}, s32[8]{0:T(128)}, u32[]{:S(2)}) copy-start(s32[8]{0:T(128)} %param.11) | copy-start | bytes 100
  5.3 39.8 %collective-permute-start = (bf16[3,4,8,16,384]{4,3,2,1,0:T(8,128)(2,1)S(1)}, bf16[3,4,8,16,384]{4,3,2,1,0:T(8,128)(2,1)S(1)}, u32[]{:S(2)}, u32[]{:S(2)}) collective-permute-start(bf16[3,4,8,16,384]{4,3,2,1,0:T(8,128)(2,1)S(1)} %bitcast.92), channel_id=1, source_target_pairs={{0,508},{4,0},{8,4},{12,8},{16,12},{20,16},{24,20},{28,24},{32,28}... | collective-permute-start | bytes 3538952 | tf_op jit(solution)/shard_map/ppermute | solution.py:19
  55.5 1.3 copy-start.2
  62.5 1.7 %copy-start.9 = (f32[4,12,64]{2,1,0:T(8,128)S(1)}, f32[4,12,64]{2,1,0:T(8,128)}, u32[]{:S(2)}) copy-start(f32[4,12,64]{2,1,0:T(8,128)} %fusion.84) | copy-start | bytes 36868
  72.9 16.2 %collective-permute-start.1 = (bf16[4,8,16,384]{3,2,1,0:T(8,128)(2,1)S(1)}, bf16[4,8,16,384]{3,2,1,0:T(8,128)(2,1)S(1)}, u32[]{:S(2)}, u32[]{:S(2)}) collective-permute-start(bf16[4,8,16,384]{3,2,1,0:T(8,128)(2,1)S(1)} %constant_dynamic-update-slice_fusion), channel_id=1, source_target_pairs={{0,4},{4,8},{8,12},{12,16},{16,20},{20,24},{24,28},{28,32},{32,36}... | collective-permute-start | bytes 1179656 | tf_op jit(solution)/shard_map/ppermute | solution.py:19
  77.4 12.1 %copy-start.1 = (bf16[4,8,16,384]{3,2,1,0:T(8,128)(2,1)S(1)}, bf16[4,8,16,384]{3,2,1,0:T(8,128)(2,1)}, u32[]{:S(2)}) copy-start(bf16[4,8,16,384]{3,2,1,0:T(8,128)(2,1)} %param.10) | copy-start | bytes 1179652
  77.5 12.1 %copy-start.5 = (bf16[384,384]{1,0:T(8,128)(2,1)S(1)}, bf16[384,384]{1,0:T(8,128)(2,1)}, u32[]{:S(2)}) copy-start(bf16[384,384]{1,0:T(8,128)(2,1)} %param.15) | copy-start | bytes 884740
  105.3 1.4 copy-start.3
  131.3 2.3 %copy-start.4 = (bf16[384,384]{1,0:T(8,128)(2,1)S(1)}, bf16[384,384]{1,0:T(8,128)(2,1)}, u32[]{:S(2)}) copy-start(bf16[384,384]{1,0:T(8,128)(2,1)} %param.17) | copy-start | bytes 884740
  133.5 1.8 %copy-start.8 = (bf16[768,384]{1,0:T(8,128)(2,1)S(1)}, bf16[768,384]{1,0:T(8,128)(2,1)}, u32[]{:S(2)}) copy-start(bf16[768,384]{1,0:T(8,128)(2,1)} %param.19) | copy-start | bytes 1769476
  138.5 12.5 %all-to-all-start.1 = ((bf16[16,8,4,384]{3,2,1,0:T(4,128)(2,1)}), bf16[16,8,4,384]{3,2,1,0:T(4,128)(2,1)S(1)}, u32[]{:S(2)}, u32[]{:S(2)}) async-start(bf16[16,8,4,384]{3,2,1,0:T(4,128)(2,1)} %reshape_reshape.4), calls=%async_computation.1 | async-start | bytes 786432 | tf_op jit(solution)/shard_map/all_to_all | solution.py:173
where the time goes:
time: 153 us; the launch traced here: 152 us
  waiting for transfers between devices  37 us (24%)
  local copies, waits for them, and re-layouts  32.7 us (21%)
  matrix products  28.2 us (18%)
  starting transfers between devices  21.5 us (14%)
  blocking collectives  14.1 us (9%)
  other arithmetic  10.6 us (7%)
  between operations  8.03 us (5%)
    ppermute x2, waiting for transfers between devices, from_behind(): return lax.ppermute(value, axis, pairs)  29 us
    ppermute x2, starting transfers between devices, from_behind(): return lax.ppermute(value, axis, pairs)  17.1 us
    all_to_all x1, blocking collectives, local(): lax.all_to_all(resident, 'lev', split_axis=2, concat_axis=0, tiled=True)  14.1 us
    all_to_all x1, waiting for transfers between devices, local(): lax.all_to_all(finished, 'lev', split_axis=0, concat_axis=2, tiled=True)  8 us
    another operation x6, local copies, waits for them, and re-layouts, to_windows(): tensor.reshape(level_count, row_count, windows, WIN_LON, HEADS, head_size)  7.85 us
    dot_general x2, matrix products, window_attend(): jnp.einsum('lnhqk,lnhkd->lnhqd', weights_bf, to_windows(values_in), prefe...  5.01 us
    dot_general x1, matrix products, column_finish(): jnp.einsum('nhqk,knhd->qnhd', weights_bf, split_v, preferred_element_type...  4.98 us
    dot_general x2, matrix products, window_attend(): jnp.einsum('lnhqd,lnhkd->lnhqk', to_windows(queries), to_windows(keys_in)...  4.63 us
  transfers between devices with their start and end apart: 3, of which 3 were waited for; matrix products, arithmetic and copies ran while one was open for 2% of the time, Pallas kernels for 0%

commit v1 on v0

v1 whole, which is shorter than its diff:
```python
import functools
import math

import jax
import jax.numpy as jnp
from jax import lax
from jax.experimental import pallas as pl
from jax.experimental.pallas import tpu as pltpu
from jax.sharding import PartitionSpec as P

HEADS = 12
WIN_ROWS = 4
WIN_LON = 16
EPSILON = 1e-05
LANES = 128
F32 = jnp.float32
BF16 = jnp.bfloat16


def move(value, axis, steps):
    count = lax.axis_size(axis)
    pairs = [(source, (source + steps) % count) for source in range(count)]
    return lax.ppermute(value, axis, pairs)


def layer_norm(values, gain_row):
    average = jnp.mean(values, axis=-1, keepdims=True)
    centred = values - average
    variance = jnp.mean(centred * centred, axis=-1, keepdims=True)
    return (centred * lax.rsqrt(variance + EPSILON) * gain_row).astype(BF16)


def dot32(left, right):
    return jnp.dot(left, right, preferred_element_type=F32)


def attend(queries, keys, values, allowed, head_size):
    count, width = queries.shape
    per = LANES // head_size
    scale = math.log2(math.e) / math.sqrt(head_size)
    head_of_lane = lax.broadcasted_iota(jnp.int32, (count, LANES), 1) // head_size
    ones = jnp.ones((keys.shape[0], LANES), BF16)
    pieces = []
    for group in range(width // LANES):
        at = slice(group * LANES, (group + 1) * LANES)
        part = queries[:, at]
        spread = jnp.concatenate(
            [jnp.where(head_of_lane == head, part, jnp.zeros_like(part)) for head in range(per)],
            axis=0,
        )
        scores = lax.dot_general(
            spread, keys[:, at], (((1,), (1,)), ((), ())), preferred_element_type=F32
        ).reshape(per, count, -1)
        scores = jnp.where(allowed[None], scores, -jnp.inf)
        highest = jnp.max(scores, axis=-1, keepdims=True)
        weights = jnp.exp2((scores - highest) * scale).astype(BF16).reshape(per * count, -1)
        mixed = dot32(weights, jnp.concatenate([values[:, at], ones], axis=1))
        mixed = mixed.reshape(per, count, 2 * LANES)
        picked = mixed[0]
        both = jnp.concatenate([head_of_lane, head_of_lane], axis=1)
        for head in range(1, per):
            picked = jnp.where(both == head, mixed[head], picked)
        pieces.append((picked[:, :LANES] / picked[:, LANES:]).astype(BF16))
    return jnp.concatenate(pieces, axis=1)


def count_of_row(counts_ref, first_row, rows):
    wanted = jnp.full(rows.shape, counts_ref[first_row], jnp.int32)
    for row in range(1, WIN_ROWS):
        wanted = jnp.where(rows == row, counts_ref[first_row + row], wanted)
    return wanted


def edge_block(shifts_ref):
    return jnp.where(shifts_ref[0] == WIN_LON - 1, 0, 1)


def window_edge_kernel(
    circle, shifts_ref, counts_ref, anchor_ref, fields_ref, cell_ref, gains_ref, qkv_ref, out_w_ref, result_ref
):
    levels, _, tokens, width = fields_ref.shape
    block = edge_block(shifts_ref)
    anchor = anchor_ref[0]
    own = fields_ref[:, block].reshape(levels * tokens, width).astype(F32)
    cells = cell_ref[...].astype(F32)
    behind = jnp.concatenate(
        [jnp.broadcast_to(cells[n : n + 1], (WIN_LON, width)) for n in range(levels * WIN_ROWS)], axis=0
    )
    place = lax.broadcasted_iota(jnp.int32, own.shape, 0) % WIN_LON
    own = jnp.where(place == WIN_LON - 1, behind, own)
    normed = layer_norm(own, gains_ref[0:1])
    queries, keys, values = [dot32(normed, qkv_ref[n]).astype(BF16) for n in range(3)]

    key = lax.broadcasted_iota(jnp.int32, (tokens, tokens), 1)
    where = key % WIN_LON
    cell = jnp.where(where == WIN_LON - 1, lax.rem(anchor + circle - 1, circle), anchor + where)
    allowed = cell < count_of_row(counts_ref, block * WIN_ROWS, key // WIN_LON)
    mixed = []
    for level in range(levels):
        at = slice(level * tokens, (level + 1) * tokens)
        mixed.append(attend(queries[at], keys[at], values[at], allowed, width // HEADS))
    mixed = jnp.concatenate(mixed, axis=0)
    result_ref[...] = (own + dot32(mixed, out_w_ref[...])).astype(BF16)


def window_both_kernel(
    circle, shifts_ref, counts_ref, anchor_ref, fields_ref, behind_ref, ahead_ref, gains_ref, qkv_ref, out_w_ref,
    result_ref,
):
    levels, _, tokens, width = fields_ref.shape
    block = 1 - edge_block(shifts_ref)
    shift = shifts_ref[block]
    anchor = anchor_ref[0]
    own = fields_ref[:, block].reshape(levels * tokens, width).astype(F32)
    place = lax.broadcasted_iota(jnp.int32, own.shape, 0) % WIN_LON
    other = jnp.where(place < shift, ahead_ref[...].astype(F32), behind_ref[...].astype(F32))
    normed_own = layer_norm(own, gains_ref[0:1])
    normed_other = layer_norm(other, gains_ref[0:1])
    queries = dot32(normed_own, qkv_ref[0]).astype(BF16)
    normed = jnp.concatenate(
        [
            part[level * tokens : (level + 1) * tokens]
            for level in range(levels)
            for part in (normed_own, normed_other)
        ],
        axis=0,
    )
    keys, values = [dot32(normed, qkv_ref[n]).astype(BF16) for n in (1, 2)]

    shape = (tokens, 2 * tokens)
    query_place = lax.broadcasted_iota(jnp.int32, shape, 0) % WIN_LON
    key = lax.broadcasted_iota(jnp.int32, shape, 1)
    where = key % WIN_LON
    here = key < tokens
    cell = anchor + where
    away = jnp.where(where < shift, cell + WIN_LON, cell - WIN_LON + circle)
    cell = jnp.where(here, cell, jnp.where(away >= circle, away - circle, away))
    rows = (key // WIN_LON) % WIN_ROWS
    same = (query_place < shift) == (where < shift)
    allowed = (here == same) & (cell < count_of_row(counts_ref, block * WIN_ROWS, rows))
    mixed = []
    for level in range(levels):
        at = slice(level * tokens, (level + 1) * tokens)
        both = slice(2 * level * tokens, 2 * (level + 1) * tokens)
        mixed.append(attend(queries[at], keys[both], values[both], allowed, width // HEADS))
    mixed = jnp.concatenate(mixed, axis=0)
    result_ref[...] = (own + dot32(mixed, out_w_ref[...])).astype(BF16)


def column_block(core_ref, gathered_ref, gains_ref, qkv_ref, out_w_ref, in_ref, mlp_ref, normed_ref):
    _, tokens, width = gathered_ref.shape
    total = gathered_ref.shape[0] * tokens
    mine = core_ref[0] * 2
    resident = gathered_ref[mine].astype(F32)
    normed = layer_norm(gathered_ref[...].reshape(total, width).astype(F32), gains_ref[1:2])
    normed_ref[...] = normed.reshape(normed_ref.shape)
    queries = dot32(normed_ref[mine], qkv_ref[0]).astype(BF16)
    keys, values = [dot32(normed, qkv_ref[n]).astype(BF16) for n in (1, 2)]

    span = WIN_ROWS * WIN_LON
    levels = tokens // span
    all_levels = total // span
    queries = queries.reshape(levels, WIN_ROWS, WIN_LON, width)
    keys = keys.reshape(all_levels, WIN_ROWS, WIN_LON, width)
    values = values.reshape(all_levels, WIN_ROWS, WIN_LON, width)
    shape = (levels * WIN_LON, all_levels * WIN_LON)
    allowed = (
        lax.broadcasted_iota(jnp.int32, shape, 0) % WIN_LON
        == lax.broadcasted_iota(jnp.int32, shape, 1) % WIN_LON
    )
    rows = []
    for row in range(WIN_ROWS):
        mixed = attend(
            queries[:, row].reshape(levels * WIN_LON, width),
            keys[:, row].reshape(all_levels * WIN_LON, width),
            values[:, row].reshape(all_levels * WIN_LON, width),
            allowed,
            width // HEADS,
        )
        rows.append(mixed.reshape(levels, 1, WIN_LON, width))
    mixed = jnp.concatenate(rows, axis=1).reshape(tokens, width)
    updated = (resident + dot32(mixed, out_w_ref[...])).astype(BF16)
    normed = layer_norm(updated.astype(F32), gains_ref[2:3])
    inner = jax.nn.gelu(dot32(normed, in_ref[...])).astype(BF16)
    return (updated.astype(F32) + dot32(inner, mlp_ref[...])).astype(BF16)


def column_edge_kernel(
    core_ref, gathered_ref, gains_ref, qkv_ref, out_w_ref, in_ref, mlp_ref, result_ref, cell_ref, normed_ref
):
    result = column_block(core_ref, gathered_ref, gains_ref, qkv_ref, out_w_ref, in_ref, mlp_ref, normed_ref)
    result_ref[...] = result
    wide = result.astype(F32)
    last = [wide[n * WIN_LON + WIN_LON - 1 : (n + 1) * WIN_LON] for n in range(cell_ref.shape[0])]
    cell_ref[...] = jnp.concatenate(last, axis=0).astype(BF16)


def column_both_kernel(
    core_ref, shifts_ref, counts_ref, anchor_ref, gathered_ref, edge_ref, cell_ref, gains_ref, qkv_ref, out_w_ref,
    in_ref, mlp_ref, result_ref, normed_ref,
):
    levels, _, tokens, width = result_ref.shape
    block = edge_block(shifts_ref)
    anchor = anchor_ref[0]
    shape = (tokens, width)
    token = lax.broadcasted_iota(jnp.int32, shape, 0)
    place = token % WIN_LON
    edge = edge_ref[...].astype(F32)
    cells = cell_ref[...].astype(F32)
    result = column_block(core_ref, gathered_ref, gains_ref, qkv_ref, out_w_ref, in_ref, mlp_ref, normed_ref)
    result = result.astype(F32)
    live_edge = anchor + place < count_of_row(counts_ref, block * WIN_ROWS, token // WIN_LON)
    live = anchor + place < count_of_row(counts_ref, (1 - block) * WIN_ROWS, token // WIN_LON)
    for level in range(levels):
        at = slice(level * tokens, (level + 1) * tokens)
        last = jnp.concatenate(
            [
                jnp.broadcast_to(cells[n : n + 1], (WIN_LON, width))
                for n in range(level * WIN_ROWS, (level + 1) * WIN_ROWS)
            ],
            axis=0,
        )
        merged = jnp.where(place == WIN_LON - 1, last, edge[at])
        result_ref[level, block] = jnp.where(live_edge, merged, 0.0).astype(BF16)
        result_ref[level, 1 - block] = jnp.where(live, result[at], 0.0).astype(BF16)


def call(body, outs, scalars, arrays, flops, scratch=()):
    smem = pl.BlockSpec(memory_space=pltpu.SMEM)
    vmem = pl.BlockSpec(memory_space=pltpu.VMEM)
    moved = sum(math.prod(a.shape) * a.dtype.itemsize for a in arrays)
    single = len(outs) == 1
    return pl.pallas_call(
        body,
        out_shape=outs[0] if single else outs,
        in_specs=[smem] * len(scalars) + [vmem] * len(arrays),
        out_specs=vmem if single else [vmem] * len(outs),
        scratch_shapes=scratch,
        compiler_params=pltpu.CompilerParams(vmem_limit_bytes=32 * 1024 * 1024),
        cost_estimate=pl.CostEstimate(flops=flops, bytes_accessed=moved, transcendentals=0),
    )(*scalars, *arrays)


def local(
    fields,
    counts,
    shifts,
    norm_gains,
    window_qkv,
    window_out,
    column_qkv,
    column_out,
    mlp_in,
    mlp_out,
):
    levels, row_count, cells, width = fields.shape
    tokens = WIN_ROWS * cells
    circle = cells * lax.axis_size("lon")
    anchor = (lax.axis_index("lon") * cells).astype(jnp.int32).reshape(1)
    core = (lax.axis_index("lev") % 2).astype(jnp.int32).reshape(1)
    blocked = fields.reshape(levels, row_count // WIN_ROWS, WIN_ROWS, cells, width)
    edge = jnp.where(shifts[0] == WIN_LON - 1, 0, 1)
    edge_cells = lax.dynamic_index_in_dim(blocked, edge, 1, keepdims=False)[:, :, cells - 1]
    whole = lax.dynamic_index_in_dim(blocked, 1 - edge, 1, keepdims=False).reshape(-1, width)
    sent_east = jnp.concatenate([edge_cells.reshape(-1, width), whole], axis=0)
    from_behind = move(sent_east, "lon", 1)
    from_ahead = move(whole, "lon", -1)
    cell_count = levels * WIN_ROWS
    behind_cells, behind = from_behind[:cell_count], from_behind[cell_count:]

    blocked = fields.reshape(levels, row_count // WIN_ROWS, tokens, width)
    one = jax.ShapeDtypeStruct((levels * tokens, width), BF16)
    resident_edge = call(
        functools.partial(window_edge_kernel, circle),
        [one],
        [shifts, counts, anchor],
        [blocked, behind_cells, norm_gains, window_qkv, window_out],
        10**9,
    )
    resident_both = call(
        functools.partial(window_both_kernel, circle),
        [one],
        [shifts, counts, anchor],
        [blocked, behind, from_ahead, norm_gains, window_qkv, window_out],
        10**9,
    )

    groups = [[0, 1], [2, 3]]
    swap = [(n, n ^ 2) for n in range(4)]

    def gather(resident):
        other = lax.ppermute(resident, "lev", swap)
        pair = jnp.stack([resident, other])
        return lax.all_gather(pair, "lev", tiled=True, axis_index_groups=groups)

    scratch = [pltpu.VMEM((4, levels * tokens, width), BF16)]
    weights = [norm_gains, column_qkv, column_out, mlp_in, mlp_out]
    edge_result, edge_last = call(
        column_edge_kernel,
        [one, jax.ShapeDtypeStruct((cell_count, width), BF16)],
        [core],
        [gather(resident_edge)] + weights,
        10**9,
        scratch,
    )
    last_cells = move(edge_last, "lon", -1)
    result = call(
        column_both_kernel,
        [jax.ShapeDtypeStruct(blocked.shape, BF16)],
        [core, shifts, counts, anchor],
        [gather(resident_both), edge_result, last_cells] + weights,
        10**9,
        scratch,
    )
    return result.reshape(fields.shape)


def solution(mesh):
    return jax.shard_map(
        local,
        mesh=mesh,
        in_specs=(P("lev", None, "lon", None), P(), P(), P(), P(), P(), P(), P(), P(), P()),
        out_specs=P("lev", None, "lon", None),
        check_vma=False,
    )
```

time: 153 us -> 55.8 us (0.36)
  waiting for transfers between devices: 37 us -> 2.94 us
  local copies, waits for them, and re-layouts: 32.7 us -> 2.52 us
  matrix products: 28.2 us -> 0 us
  Pallas kernels: 0 us -> 15.6 us
  other arithmetic: 10.6 us -> 0.12 us
  between operations: 8.03 us -> 0.28 us
  blocking collectives: 14.1 us -> 6.87 us
  starting transfers between devices: 21.5 us -> 27.2 us
    ppermute x2 -> x5, waiting for transfers between devices: 29 us -> 2.94 us  [the longest x3 2.93 us: move(): return lax.ppermute(value, axis, pairs)]
    dot_general x11 -> x0, matrix products: 24.6 us -> none  [the longest x2 5.01 us: window_attend(): jnp.einsum('lnhqk,lnhkd->lnhqd', weights_bf, to_windows(values_in), prefe...]
    another operation x10 -> x1, local copies, waits for them, and re-layouts: 16.4 us -> 0.01 us  [local(): sent_east = jnp.concatenate([edge_cells.reshape(-1, width), whole], axis=0)]
    pallas_call x0 -> x4, Pallas kernels: none -> 15.6 us  [call(): pl.pallas_call(body, out_shape=outs[0] if single else outs, in_specs=[sme...]
    all_to_all x1 -> x0, blocking collectives: 14.1 us -> none  [local(): lax.all_to_all(resident, 'lev', split_axis=2, concat_axis=0, tiled=True)]
    ppermute x2 -> x5, starting transfers between devices: 17.1 us -> 27.2 us  [the longest x3 20.5 us: move(): return lax.ppermute(value, axis, pairs)]
    all_to_all x1 -> x0, waiting for transfers between devices: 8 us -> none  [local(): lax.all_to_all(finished, 'lev', split_axis=0, concat_axis=2, tiled=True)]
    all_gather x0 -> x2, blocking collectives: none -> 6.87 us  [gather(): return lax.all_gather(pair, 'lev', tiled=True, axis_index_groups=groups)]
  transfers between devices with their start and end apart: 3 -> 5, of which waited for: 3 -> 1; matrix products, arithmetic and copies ran while one was open for 2% -> 0% of each run, Pallas kernels for 0% -> 19%
where the time goes in v1:
time: 55.8 us; the launch traced here: 55.5 us
  starting transfers between devices  27.2 us (49%)
  Pallas kernels  15.6 us (28%)
  blocking collectives  6.87 us (12%)
  waiting for transfers between devices  2.94 us (5%)
  local copies, waits for them, and re-layouts  2.52 us (5%)
    ppermute x3, starting transfers between devices, move(): return lax.ppermute(value, axis, pairs)  20.5 us
    pallas_call x4, Pallas kernels, call(): pl.pallas_call(body, out_shape=outs[0] if single else outs, in_specs=[sme...  15.6 us
    all_gather x2, blocking collectives, gather(): return lax.all_gather(pair, 'lev', tiled=True, axis_index_groups=groups)  6.87 us
    ppermute x2, starting transfers between devices, gather(): other = lax.ppermute(resident, 'lev', swap)  6.79 us
    ppermute x3, waiting for transfers between devices, move(): return lax.ppermute(value, axis, pairs)  2.93 us
    unnamed x20, local copies, waits for them, and re-layouts  1.33 us
    dynamic_slice x2, local copies, waits for them, and re-layouts, local(): lax.dynamic_index_in_dim(blocked, edge, 1, keepdims=False)[:, :, cells - 1]  1.15 us
  transfers between devices with their start and end apart: 5, of which 1 were waited for; matrix products, arithmetic and copies ran while one was open for 0% of the time, Pallas kernels for 19%

profile of v1, /device:TPU:1, one launch (start us, length us, event | category | flops | bytes accessed | tf_op | source)
XLA Modules:
  0.0 55.5 jit_solution(10346735570889749972)
XLA Ops:
  0.0 0.0 copy-start.6
  0.0 0.0 copy-start.8
  0.0 0.7 %copy-done.6 = s32[2]{0:T(128)S(1)} copy-done((s32[2]{0:T(128)S(1)}, s32[2]{0:T(128)}, u32[]{:S(2)}) %copy-start.6) | copy-done | bytes 32
  0.7 1.1 %constant_dynamic-slice_fusion.1 = (bf16[4,1,4,16,384]{4,3,2,1,0:T(8,128)(2,1)S(1)}, bf16[4,1,4,16,384]{4,3,2,1,0:T(8,128)(2,1)S(1)}) fusion(bf16[4,2,4,16,384]{4,3,2,1,0:T(8,128)(2,1)} %bitcast.19, s32[]{:T(128)} %bitcast.4, s32[]{:T(128)S(6)} %select_n.22), kind=kLoop, calls=%fused_computation.5 | loop fusion | bytes 786440 | tf_op jit(solution)/shard_map/jit(dynamic_index_in_dim)/dynamic_slice | solution.py:263
  1.8 0.0 copy-start.3
  1.8 0.1 copy.17
  1.9 0.0 copy-start.9
  1.9 4.2 %collective-permute-start = (bf16[272,384]{1,0:T(8,128)(2,1)S(1)}, bf16[272,384]{1,0:T(8,128)(2,1)S(1)}, u32[]{:S(2)}, u32[]{:S(2)}) collective-permute-start(bf16[272,384]{1,0:T(8,128)(2,1)S(1)} %pad_maximum_fusion.2), channel_id=1, source_target_pairs={{0,4},{4,8},{8,12},{12,16},{16,20},{20,24},{24,28},{28,32},{32,36}... | collective-permute-start | bytes 626696 | tf_op jit(solution)/shard_map/ppermute | solution.py:23
  6.1 13.0 %collective-permute-start.1 = (bf16[256,384]{1,0:T(8,128)(2,1)S(1)}, bf16[256,384]{1,0:T(8,128)(2,1)S(1)}, u32[]{:S(2)}, u32[]{:S(2)}) collective-permute-start(bf16[256,384]{1,0:T(8,128)(2,1)S(1)} %bitcast.26), channel_id=1, source_target_pairs={{0,508},{4,0},{8,4},{12,8},{16,12},{20,16},{24,20},{28,24},{32,28}... | collective-permute-start | bytes 589832 | tf_op jit(solution)/shard_map/ppermute | solution.py:23
  19.2 0.0 copy-start.5
  19.2 2.9 %collective-permute-done = bf16[272,384]{1,0:T(8,128)(2,1)S(1)} collective-permute-done((bf16[272,384]{1,0:T(8,128)(2,1)S(1)}, bf16[272,384]{1,0:T(8,128)(2,1)S(1)}, u32[]{:S(2)}, u32[]{:S(2)}) %collective-permute-start) | collective-permute-done | bytes 208928 | tf_op jit(solution)/shard_map/ppermute | solution.py:23
  22.1 0.0 copy-start.7
  22.1 0.0 copy-done.8
  22.1 0.0 copy-done.3
  22.1 0.0 copy-done.9
  22.1 0.0 copy-done.5
  22.2 0.6 %copy-done.7 = s32[8]{0:T(128)S(1)} copy-done((s32[8]{0:T(128)S(1)}, s32[8]{0:T(128)}, u32[]{:S(2)}) %copy-start.7) | copy-done | bytes 56
  22.8 3.1 %shard_map.101 = bf16[256,384]{1,0:T(8,128)(2,1)S(1)} custom-call(s32[2]{0:T(128)S(1)} %copy-done.6, s32[8]{0:T(128)S(1)} %copy-done.7, s32[1]{0:T(128)} %bitcast.1.anchor_ref, bf16[4,2,64,384]{3,2,1,0:T(8,128)(2,1)S(1)} %bitcast.20, bf16[16,384]{1,0:T(8,128)(2,1)S(1)} %slice.18.cell_ref, f32[3,384]{1,0:T(4,128)S(1)} %copy-done.5, ...), custom_call_target="tpu_custom_call" | custom-call | flops 1000000000 | bytes 1589760 | tf_op jit(solution)/shard_map/pallas_call | solution.py:233
  25.9 4.5 %collective-permute-start.3 = (bf16[256,384]{1,0:T(8,128)(2,1)S(1)}, bf16[256,384]{1,0:T(8,128)(2,1)S(1)}, u32[]{:S(2)}, u32[]{:S(2)}) collective-permute-start(bf16[256,384]{1,0:T(8,128)(2,1)S(1)} %shard_map.101), channel_id=1, source_target_pairs={{0,2},{1,3},{2,0},{3,1},{4,6},{5,7},{6,4},{7,5},{8,10},{9,11},{10,... | collective-permute-start | bytes 589832 | tf_op jit(solution)/shard_map/ppermute | solution.py:292
  30.5 0.0 collective-permute-done.1.ahead_ref
  30.5 0.0 copy-start.2
  30.5 3.5 %shard_map.100 = bf16[256,384]{1,0:T(8,128)(2,1)S(1)} custom-call(s32[2]{0:T(128)S(1)} %copy-done.6, s32[8]{0:T(128)S(1)} %copy-done.7, s32[1]{0:T(128)} %bitcast.1.anchor_ref, bf16[4,2,64,384]{3,2,1,0:T(8,128)(2,1)S(1)} %bitcast.21, bf16[256,384]{1,0:T(8,128)(2,1)S(1)} %slice.17.behind_ref, bf16[256,384]{1,0:T(8,128)(2,1)S(1)} %collective-permute-done.1.ahead_ref, ...), custom_call_target="tpu_custom_call" | custom-call | flops 1000000000 | bytes 1970688 | tf_op jit(solution)/shard_map/pallas_call | solution.py:233
  34.0 2.3 %collective-permute-start.2 = (bf16[256,384]{1,0:T(8,128)(2,1)S(1)}, bf16[256,384]{1,0:T(8,128)(2,1)S(1)}, u32[]{:S(2)}, u32[]{:S(2)}) collective-permute-start(bf16[256,384]{1,0:T(8,128)(2,1)S(1)} %shard_map.100), channel_id=1, source_target_pairs={{0,2},{1,3},{2,0},{3,1},{4,6},{5,7},{6,4},{7,5},{8,10},{9,11},{10,... | collective-permute-start | bytes 589832 | tf_op jit(solution)/shard_map/ppermute | solution.py:292
  36.3 0.0 collective-permute-done.3
  36.3 0.0 copy-start
  36.4 0.0 copy-start.1
  36.4 0.0 copy-start.4
  36.4 4.0 %all_gather.7.gathered_ref = bf16[4,256,384]{2,1,0:T(8,128)(2,1)S(1)} all-gather(bf16[2,256,384]{2,1,0:T(8,128)(2,1)S(1)} %pad_maximum_fusion.1), channel_id=1, replica_groups={{0,1},{2,3},{4,5},{6,7},{8,9},{10,11},{12,13},{14,15},{16,17},{18,19},{..., dimensions={0}, use_global_device_ids=true | all-gather | bytes 1179648 | tf_op jit(solution)/shard_map/all_gather | solution.py:294
  40.4 0.0 copy-done.2
  40.5 0.0 copy-done
  40.5 0.0 copy-done.1
  40.5 0.0 copy-done.4
  40.5 3.8 %shard_map.102 = (bf16[256,384]{1,0:T(8,128)(2,1)S(1)}, bf16[16,384]{1,0:T(8,128)(2,1)S(1)}) custom-call(s32[1]{0:T(128)} %bitcast.core_ref, bf16[4,256,384]{2,1,0:T(8,128)(2,1)S(1)} %all_gather.7.gathered_ref, f32[3,384]{1,0:T(4,128)S(1)} %copy-done.5, bf16[3,384,384]{2,1,0:T(8,128)(2,1)S(1)} %copy-done, bf16[384,384]{1,0:T(8,128)(2,1)S(1)} %copy-done.4, ...), custom_call_target="tpu_custom_call" | custom-call | flops 1000000000 | bytes 3150336 | tf_op jit(solution)/shard_map/pallas_call | solution.py:233
  44.3 3.2 %collective-permute-start.4 = (bf16[16,384]{1,0:T(8,128)(2,1)S(1)}, bf16[16,384]{1,0:T(8,128)(2,1)S(1)}, u32[]{:S(2)}, u32[]{:S(2)}) collective-permute-start(bf16[16,384]{1,0:T(8,128)(2,1)S(1)} %get-tuple-element.8), channel_id=1, source_target_pairs={{0,508},{4,0},{8,4},{12,8},{16,12},{20,16},{24,20},{28,24},{32,28}... | collective-permute-start | bytes 36872 | tf_op jit(solution)/shard_map/ppermute | solution.py:23
  47.5 0.0 collective-permute-done.2
  47.6 2.8 %all_gather.6.gathered_ref = bf16[4,256,384]{2,1,0:T(8,128)(2,1)S(1)} all-gather(bf16[2,256,384]{2,1,0:T(8,128)(2,1)S(1)} %pad_maximum_fusion), channel_id=1, replica_groups={{0,1},{2,3},{4,5},{6,7},{8,9},{10,11},{12,13},{14,15},{16,17},{18,19},{..., dimensions={0}, use_global_device_ids=true | all-gather | bytes 1179648 | tf_op jit(solution)/shard_map/all_gather | solution.py:294
  50.4 0.0 collective-permute-done.4.cell_ref
  50.4 5.1 %shard_map.103 = bf16[4,2,64,384]{3,2,1,0:T(8,128)(2,1)} custom-call(s32[1]{0:T(128)} %bitcast.core_ref, s32[2]{0:T(128)S(1)} %copy-done.6, s32[8]{0:T(128)S(1)} %copy-done.7, s32[1]{0:T(128)} %bitcast.1.anchor_ref, bf16[4,256,384]{2,1,0:T(8,128)(2,1)S(1)} %all_gather.6.gathered_ref, bf16[256,384]{1,0:T(8,128)(2,1)S(1)} %get-tuple-element.7.edge_ref, ...), custom_call_target="tpu_custom_call" | custom-call | flops 1000000000 | bytes 3359232 | tf_op jit(solution)/shard_map/pallas_call | solution.py:233
  (7 shorter events, 0.2 us)
Async XLA Ops:
  0.0 0.7 %copy-start.6 = (s32[2]{0:T(128)S(1)}, s32[2]{0:T(128)}, u32[]{:S(2)}) copy-start(s32[2]{0:T(128)} %shifts_ref.5) | copy-start | bytes 28
  0.0 22.1 %copy-start.8 = (bf16[3,384,384]{2,1,0:T(8,128)(2,1)S(1)}, bf16[3,384,384]{2,1,0:T(8,128)(2,1)}, u32[]{:S(2)}) copy-start(bf16[3,384,384]{2,1,0:T(8,128)(2,1)} %qkv_ref.5) | copy-start | bytes 2654212
  1.8 20.4 %copy-start.3 = (bf16[4,8,16,384]{3,2,1,0:T(8,128)(2,1)S(1)}, bf16[4,8,16,384]{3,2,1,0:T(8,128)(2,1)}, u32[]{:S(2)}) copy-start(bf16[4,8,16,384]{3,2,1,0:T(8,128)(2,1)} %param.10) | copy-start | bytes 1179652
  1.9 20.3 %copy-start.9 = (bf16[384,384]{1,0:T(8,128)(2,1)S(1)}, bf16[384,384]{1,0:T(8,128)(2,1)}, u32[]{:S(2)}) copy-start(bf16[384,384]{1,0:T(8,128)(2,1)} %out_w_ref.5) | copy-start | bytes 884740
  1.9 20.2 %collective-permute-start = (bf16[272,384]{1,0:T(8,128)(2,1)S(1)}, bf16[272,384]{1,0:T(8,128)(2,1)S(1)}, u32[]{:S(2)}, u32[]{:S(2)}) collective-permute-start(bf16[272,384]{1,0:T(8,128)(2,1)S(1)} %pad_maximum_fusion.2), channel_id=1, source_target_pairs={{0,4},{4,8},{8,12},{12,16},{16,20},{20,24},{24,28},{28,32},{32,36}... | collective-permute-start | bytes 626696 | tf_op jit(solution)/shard_map/ppermute | solution.py:23
  6.1 24.4 %collective-permute-start.1 = (bf16[256,384]{1,0:T(8,128)(2,1)S(1)}, bf16[256,384]{1,0:T(8,128)(2,1)S(1)}, u32[]{:S(2)}, u32[]{:S(2)}) collective-permute-start(bf16[256,384]{1,0:T(8,128)(2,1)S(1)} %bitcast.26), channel_id=1, source_target_pairs={{0,508},{4,0},{8,4},{12,8},{16,12},{20,16},{24,20},{28,24},{32,28}... | collective-permute-start | bytes 589832 | tf_op jit(solution)/shard_map/ppermute | solution.py:23
  19.2 3.0 %copy-start.5 = (f32[3,384]{1,0:T(4,128)S(1)}, f32[3,384]{1,0:T(4,128)}, u32[]{:S(2)}) copy-start(f32[3,384]{1,0:T(4,128)} %gains_ref.7) | copy-start | bytes 13828
  22.1 0.7 %copy-start.7 = (s32[8]{0:T(128)S(1)}, s32[8]{0:T(128)}, u32[]{:S(2)}) copy-start(s32[8]{0:T(128)} %counts_ref.5) | copy-start | bytes 100
  25.9 10.4 %collective-permute-start.3 = (bf16[256,384]{1,0:T(8,128)(2,1)S(1)}, bf16[256,384]{1,0:T(8,128)(2,1)S(1)}, u32[]{:S(2)}, u32[]{:S(2)}) collective-permute-start(bf16[256,384]{1,0:T(8,128)(2,1)S(1)} %shard_map.101), channel_id=1, source_target_pairs={{0,2},{1,3},{2,0},{3,1},{4,6},{5,7},{6,4},{7,5},{8,10},{9,11},{10,... | collective-permute-start | bytes 589832 | tf_op jit(solution)/shard_map/ppermute | solution.py:292
  30.5 10.0 %copy-start.2 = (bf16[768,384]{1,0:T(8,128)(2,1)S(1)}, bf16[768,384]{1,0:T(8,128)(2,1)}, u32[]{:S(2)}) copy-start(bf16[768,384]{1,0:T(8,128)(2,1)} %mlp_ref.3) | copy-start | bytes 1769476
  34.0 13.5 %collective-permute-start.2 = (bf16[256,384]{1,0:T(8,128)(2,1)S(1)}, bf16[256,384]{1,0:T(8,128)(2,1)S(1)}, u32[]{:S(2)}, u32[]{:S(2)}) collective-permute-start(bf16[256,384]{1,0:T(8,128)(2,1)S(1)} %shard_map.100), channel_id=1, source_target_pairs={{0,2},{1,3},{2,0},{3,1},{4,6},{5,7},{6,4},{7,5},{8,10},{9,11},{10,... | collective-permute-start | bytes 589832 | tf_op jit(solution)/shard_map/ppermute | solution.py:292
  36.3 4.1 %copy-start = (bf16[3,384,384]{2,1,0:T(8,128)(2,1)S(1)}, bf16[3,384,384]{2,1,0:T(8,128)(2,1)}, u32[]{:S(2)}) copy-start(bf16[3,384,384]{2,1,0:T(8,128)(2,1)} %qkv_ref.7) | copy-start | bytes 2654212
  36.4 4.1 %copy-start.1 = (bf16[384,768]{1,0:T(8,128)(2,1)S(1)}, bf16[384,768]{1,0:T(8,128)(2,1)}, u32[]{:S(2)}) copy-start(bf16[384,768]{1,0:T(8,128)(2,1)} %in_ref.3) | copy-start | bytes 1769476
  36.4 4.1 %copy-start.4 = (bf16[384,384]{1,0:T(8,128)(2,1)S(1)}, bf16[384,384]{1,0:T(8,128)(2,1)}, u32[]{:S(2)}) copy-start(bf16[384,384]{1,0:T(8,128)(2,1)} %out_w_ref.7) | copy-start | bytes 884740
  44.3 6.1 %collective-permute-start.4 = (bf16[16,384]{1,0:T(8,128)(2,1)S(1)}, bf16[16,384]{1,0:T(8,128)(2,1)S(1)}, u32[]{:S(2)}, u32[]{:S(2)}) collective-permute-start(bf16[16,384]{1,0:T(8,128)(2,1)S(1)} %get-tuple-element.8), channel_id=1, source_target_pairs={{0,508},{4,0},{8,4},{12,8},{16,12},{20,16},{24,20},{28,24},{32,28}... | collective-permute-start | bytes 36872 | tf_op jit(solution)/shard_map/ppermute | solution.py:23

commit v2 on v0

v2 whole, which is shorter than its diff:
```python
import functools
import math

import jax
import jax.numpy as jnp
from jax import lax
from jax.experimental import pallas as pl
from jax.experimental.pallas import tpu as pltpu
from jax.sharding import PartitionSpec as P

HEADS = 12
WIN_ROWS = 4
WIN_LON = 16
EPSILON = 1e-05
LANES = 128
CORES = 2
F32 = jnp.float32
BF16 = jnp.bfloat16


def layer_norm(values, gain_row):
    average = jnp.mean(values, axis=-1, keepdims=True)
    centred = values - average
    variance = jnp.mean(centred * centred, axis=-1, keepdims=True)
    return (centred * lax.rsqrt(variance + EPSILON) * gain_row).astype(BF16)


def dot32(left, right):
    return jnp.dot(left, right, preferred_element_type=F32)


def attend(units, allowed, head_size):
    count, width = units[0][0].shape
    per = LANES // head_size
    scale = math.log2(math.e) / math.sqrt(head_size)
    head_of_lane = lax.broadcasted_iota(jnp.int32, (count, LANES), 1) // head_size
    both = jnp.concatenate([head_of_lane, head_of_lane], axis=1)
    ones = jnp.ones((units[0][1].shape[0], LANES), BF16)
    groups = width // LANES
    cuts = [slice(group * LANES, (group + 1) * LANES) for group in range(groups)]
    jobs = [[part[:, at] for part in unit] for unit in units for at in cuts]
    scores = []
    for queries, keys, _ in jobs:
        spread = jnp.concatenate(
            [jnp.where(head_of_lane == head, queries, jnp.zeros_like(queries)) for head in range(per)], axis=0
        )
        scores.append(
            lax.dot_general(spread, keys, (((1,), (1,)), ((), ())), preferred_element_type=F32)
        )
    weights = []
    for score in scores:
        score = jnp.where(allowed[None], score.reshape(per, count, -1), -jnp.inf)
        highest = jnp.max(score, axis=-1, keepdims=True)
        weights.append(jnp.exp2((score - highest) * scale).astype(BF16).reshape(per * count, -1))
    mixes = [
        dot32(weight, jnp.concatenate([values, ones], axis=1)).reshape(per, count, 2 * LANES)
        for weight, (_, _, values) in zip(weights, jobs)
    ]
    pieces = []
    for mixed in mixes:
        picked = mixed[0]
        for head in range(1, per):
            picked = jnp.where(both == head, mixed[head], picked)
        pieces.append((picked[:, :LANES] / picked[:, LANES:]).astype(BF16))
    return [
        jnp.concatenate(pieces[first : first + groups], axis=1) for first in range(0, len(pieces), groups)
    ]


SHIFT, BOTH_COUNTS, EDGE_COUNTS, FACTS = 0, 1, 5, 16


def fact(facts_ref, row):
    return facts_ref[row : row + 1, :1]


def count_of_row(facts_ref, first, rows):
    wanted = fact(facts_ref, first)
    for row in range(1, WIN_ROWS):
        wanted = jnp.where(rows == row, fact(facts_ref, first + row), wanted)
    return wanted


def edge_block(shifts_ref):
    return jnp.where(shifts_ref[0] == WIN_LON - 1, 0, 1)


def pack_kernel(
    shifts_hbm, counts_hbm, fields_hbm, gains_hbm, qkv_hbm, out_w_hbm, east_ref, edge_ref, other_ref, facts_ref,
    gains_ref, qkv_ref, out_w_ref, shifts_ref, counts_ref, fields_ref, sems,
):
    runs, cells, width = edge_ref.shape
    moves = [
        (shifts_hbm, shifts_ref), (counts_hbm, counts_ref), (fields_hbm, fields_ref), (gains_hbm, gains_ref),
        (qkv_hbm, qkv_ref), (out_w_hbm, out_w_ref),
    ]
    copies = [pltpu.make_async_copy(*ends, sems.at[n]) for n, ends in enumerate(moves)]
    for copy in copies:
        copy.start()
    for copy in copies[:3]:
        copy.wait()
    block = edge_block(shifts_ref)
    edge = fields_ref[:, block].reshape(runs, cells, width)
    other = fields_ref[:, 1 - block].reshape(runs, cells, width)
    edge_ref[...] = edge
    other_ref[...] = east_ref[1:] = other
    edge = edge.astype(F32)
    east_ref[0] = jnp.concatenate([edge[run, cells - 1 :] for run in range(runs)], axis=0).astype(BF16)
    numbers = [shifts_ref[1 - block]]
    numbers += [counts_ref[(1 - block) * WIN_ROWS + row] for row in range(WIN_ROWS)]
    numbers += [counts_ref[block * WIN_ROWS + row] for row in range(WIN_ROWS)]
    place = lax.broadcasted_iota(jnp.int32, facts_ref.shape, 0)
    facts = jnp.zeros(facts_ref.shape, jnp.int32)
    for row, number in enumerate(numbers):
        facts = jnp.where(place == row, number, facts)
    facts_ref[...] = facts
    for copy in copies[3:]:
        copy.wait()


def window_block(
    circle, shift, counts_row, other, own, facts_ref, anchor_ref, gains_ref, qkv_ref, out_w_ref, result_ref, normed_ref
):
    total, width = own.shape
    tokens = WIN_ROWS * WIN_LON
    anchor = anchor_ref[:1, :1]
    normed = layer_norm(own, gains_ref[0:1])
    queries = dot32(normed, qkv_ref[0]).astype(BF16)
    other = layer_norm(other, gains_ref[0:1])
    normed = jnp.concatenate(
        [part[first : first + tokens] for first in range(0, total, tokens) for part in (normed, other)], axis=0
    )
    keys, values = [dot32(normed, qkv_ref[n]).astype(BF16) for n in (1, 2)]

    shape = (tokens, 2 * tokens)
    query_place = lax.broadcasted_iota(jnp.int32, shape, 0) % WIN_LON
    key = lax.broadcasted_iota(jnp.int32, shape, 1)
    where = key % WIN_LON
    here = key < tokens
    cell = anchor + where
    away = jnp.where(where < shift, cell + WIN_LON, cell - WIN_LON + circle)
    cell = jnp.where(here, cell, jnp.where(away >= circle, away - circle, away))
    same = (query_place < shift) == (where < shift)
    allowed = (here == same) & (cell < count_of_row(facts_ref, counts_row, (key // WIN_LON) % WIN_ROWS))
    units = []
    for first in range(0, total, tokens):
        both = slice(2 * first, 2 * (first + tokens))
        units.append((queries[first : first + tokens], keys[both], values[both]))
    mixed = attend(units, allowed, width // HEADS)
    resident = (own + dot32(jnp.concatenate(mixed, axis=0), out_w_ref[...])).astype(BF16)
    result_ref[...] = resident
    normed_ref[...] = layer_norm(resident.astype(F32), gains_ref[1:2])


def window_edge_kernel(
    circle, facts_ref, anchor_ref, own_ref, behind_ref, ahead_ref, gains_ref, qkv_ref, out_w_ref, _,
    result_ref, normed_ref,
):
    total, width = result_ref.shape
    cells = behind_ref[0].astype(F32)
    behind = jnp.concatenate(
        [jnp.broadcast_to(cells[n : n + 1], (WIN_LON, width)) for n in range(total // WIN_LON)], axis=0
    )
    place = lax.broadcasted_iota(jnp.int32, (total, width), 0) % WIN_LON
    other = jnp.where(place == WIN_LON - 1, behind, ahead_ref[...].reshape(total, width).astype(F32))
    window_block(
        circle, WIN_LON - 1, EDGE_COUNTS, other, own_ref[...].reshape(total, width).astype(F32), facts_ref,
        anchor_ref, gains_ref, qkv_ref, out_w_ref, result_ref, normed_ref,
    )


def window_both_kernel(
    circle, facts_ref, anchor_ref, own_ref, behind_ref, ahead_ref, gains_ref, qkv_ref, out_w_ref, result_ref,
    normed_ref,
):
    total, width = result_ref.shape
    shift = fact(facts_ref, SHIFT)
    place = lax.broadcasted_iota(jnp.int32, (total, width), 0) % WIN_LON
    behind = behind_ref[1:].reshape(total, width).astype(F32)
    ahead = ahead_ref[...].reshape(total, width).astype(F32)
    window_block(
        circle, shift, BOTH_COUNTS, jnp.where(place < shift, ahead, behind),
        own_ref[...].reshape(total, width).astype(F32), facts_ref, anchor_ref, gains_ref, qkv_ref, out_w_ref,
        result_ref, normed_ref,
    )


def column_attend(normed_ref, gathered_ref, qkv_ref):
    parts, tokens, width = gathered_ref.shape
    total = parts * tokens
    normed = gathered_ref[...].reshape(total, width)
    queries = dot32(normed_ref[...], qkv_ref[0]).astype(BF16)
    keys, values = [dot32(normed, qkv_ref[n]).astype(BF16) for n in (1, 2)]

    span = WIN_ROWS * WIN_LON
    levels = tokens // span
    all_levels = total // span
    queries = queries.reshape(levels, WIN_ROWS, WIN_LON, width)
    keys = keys.reshape(all_levels, WIN_ROWS, WIN_LON, width)
    values = values.reshape(all_levels, WIN_ROWS, WIN_LON, width)
    shape = (levels * WIN_LON, all_levels * WIN_LON)
    allowed = (
        lax.broadcasted_iota(jnp.int32, shape, 0) % WIN_LON
        == lax.broadcasted_iota(jnp.int32, shape, 1) % WIN_LON
    )
    mixed = []
    for first in range(0, WIN_ROWS, 2):
        units = [
            (
                queries[:, row].reshape(levels * WIN_LON, width),
                keys[:, row].reshape(all_levels * WIN_LON, width),
                values[:, row].reshape(all_levels * WIN_LON, width),
            )
            for row in (first, first + 1)
        ]
        mixed += attend(units, allowed, width // HEADS)
    mixed = jnp.concatenate([part.reshape(levels, 1, WIN_LON, width) for part in mixed], axis=1)
    return mixed.reshape(tokens, width)


def feed_forward(mixed, resident_ref, gains_ref, out_w_ref, in_ref, mlp_ref):
    tokens = mixed.shape[0]
    half = tokens // 2
    halves = [slice(0, half), slice(half, tokens)]
    updated = [
        (resident_ref[at].astype(F32) + dot32(mixed[at], out_w_ref[...])).astype(BF16) for at in halves
    ]
    normed = [layer_norm(part.astype(F32), gains_ref[2:3]) for part in updated]
    inner = [dot32(part, in_ref[...]) for part in normed]
    inner = [jax.nn.gelu(part).astype(BF16) for part in inner]
    result = [part.astype(F32) + dot32(act, mlp_ref[...]) for part, act in zip(updated, inner)]
    return jnp.concatenate(result, axis=0)


def live_cells(facts_ref, anchor_ref, counts_row, values):
    tokens = WIN_ROWS * WIN_LON
    width = values.shape[1]
    token = lax.broadcasted_iota(jnp.int32, (tokens, width), 0)
    live = anchor_ref[:1, :1] + token % WIN_LON < count_of_row(facts_ref, counts_row, token // WIN_LON)
    return jnp.where(live[None], values.reshape(-1, tokens, width), 0.0).astype(BF16)


def column_first_kernel(
    facts_ref, anchor_ref, resident_ref, normed_ref, gathered_ref, gains_ref, qkv_ref, out_w_ref, in_ref, mlp_ref,
    result_ref,
):
    mixed = column_attend(normed_ref, gathered_ref, qkv_ref)
    result = feed_forward(mixed, resident_ref, gains_ref, out_w_ref, in_ref, mlp_ref)
    result_ref[...] = live_cells(facts_ref, anchor_ref, BOTH_COUNTS, result)


def column_last_kernel(
    shifts_hbm, facts_ref, anchor_ref, resident_ref, normed_ref, gathered_ref, first_ref, gains_ref, qkv_ref,
    out_w_ref, in_ref, mlp_ref, result_ref, stage_ref, shifts_ref, sems,
):
    shifts_copy = pltpu.make_async_copy(shifts_hbm, shifts_ref, sems.at[2])
    shifts_copy.start()
    mixed = column_attend(normed_ref, gathered_ref, qkv_ref)
    shifts_copy.wait()
    block = edge_block(shifts_ref)
    first = pltpu.make_async_copy(first_ref, result_ref.at[:, 1 - block], sems.at[0])
    first.start()
    result = feed_forward(mixed, resident_ref, gains_ref, out_w_ref, in_ref, mlp_ref)
    stage_ref[...] = live_cells(facts_ref, anchor_ref, EDGE_COUNTS, result)
    second = pltpu.make_async_copy(stage_ref, result_ref.at[:, block], sems.at[1])
    second.start()
    first.wait()
    second.wait()


def call(body, outs, scalars, arrays, flops, scratch=(), spaces=None, out_spaces=None):
    spaces = spaces or [pltpu.VMEM] * len(arrays)
    out = [pl.BlockSpec(memory_space=space) for space in out_spaces or [pltpu.VMEM] * len(outs)]
    moved = sum(math.prod(a.shape) * a.dtype.itemsize for a in arrays)
    single = len(outs) == 1
    arrays = [
        pltpu.with_memory_space_constraint(array, space) if space == pltpu.HBM else array
        for array, space in zip(arrays, spaces)
    ]
    return pl.pallas_call(
        body,
        out_shape=outs[0] if single else outs,
        in_specs=[pl.BlockSpec(memory_space=pltpu.SMEM)] * len(scalars)
        + [pl.BlockSpec(memory_space=space) for space in spaces],
        out_specs=out[0] if single else out,
        scratch_shapes=scratch,
        compiler_params=pltpu.CompilerParams(vmem_limit_bytes=24 * 1024 * 1024),
        cost_estimate=pl.CostEstimate(flops=flops, bytes_accessed=moved, transcendentals=0),
    )(*scalars, *arrays)


def local(
    fields,
    counts,
    shifts,
    norm_gains,
    window_qkv,
    window_out,
    column_qkv,
    column_out,
    mlp_in,
    mlp_out,
):
    levels, row_count, cells, width = fields.shape
    blocks = row_count // WIN_ROWS
    tokens = WIN_ROWS * cells
    total = levels * tokens
    runs = levels * WIN_ROWS
    tiles = lax.axis_size("lon")
    circle = cells * tiles
    anchor = jnp.full((8, LANES), lax.axis_index("lon") * cells, jnp.int32)

    weights = [norm_gains, window_qkv, window_out]
    sent, edge, other, facts, *weights = call(
        pack_kernel,
        [
            jax.ShapeDtypeStruct((1 + runs, cells, width), BF16),
            jax.ShapeDtypeStruct((runs, cells, width), BF16),
            jax.ShapeDtypeStruct((runs, cells, width), BF16),
            jax.ShapeDtypeStruct((FACTS, LANES), jnp.int32),
        ]
        + [jax.ShapeDtypeStruct(array.shape, array.dtype) for array in weights],
        [],
        [shifts, counts, fields.reshape(levels, blocks, WIN_ROWS, cells, width)] + weights,
        10**6,
        [
            pltpu.SMEM(shifts.shape, jnp.int32),
            pltpu.SMEM(counts.shape, jnp.int32),
            pltpu.VMEM((levels, blocks, WIN_ROWS, cells, width), BF16),
            pltpu.SemaphoreType.DMA((6,)),
        ],
        [pltpu.HBM] * 6,
    )
    west = [(tile, (tile - 1) % tiles) for tile in range(tiles)]
    behind = lax.ppermute(sent, "lon", [pair[::-1] for pair in west])
    ahead_other = lax.ppermute(other, "lon", west)

    one = jax.ShapeDtypeStruct((total, width), BF16)
    ahead_edge = lax.ppermute(edge, "lon", west)

    resident_other, normed_other = call(
        functools.partial(window_both_kernel, circle),
        [one, one],
        [],
        [facts, anchor, other, behind, ahead_other] + weights,
        10**9,
    )
    resident_edge, normed_edge = call(
        functools.partial(window_edge_kernel, circle),
        [one, one],
        [],
        [facts, anchor, edge, behind, ahead_edge] + weights + [resident_other],
        10**9,
        spaces=[pltpu.VMEM] * (5 + len(weights)) + [pl.ANY],
    )

    groups = [[first, first + 1] for first in range(0, 2 * CORES, CORES)]
    swap = [(n, n ^ CORES) for n in range(2 * CORES)]

    def gather(part, other):
        return lax.all_gather(jnp.stack([part, other]), "lev", tiled=True, axis_index_groups=groups)

    swapped_other, swapped_edge = [lax.ppermute(part, "lev", swap) for part in (normed_other, normed_edge)]
    weights = [norm_gains, column_qkv, column_out, mlp_in, mlp_out]
    first = call(
        column_first_kernel,
        [jax.ShapeDtypeStruct((levels, tokens, width), BF16)],
        [],
        [facts, anchor, resident_other, normed_other, gather(normed_other, swapped_other)] + weights,
        10**9,
    )
    first, swapped_edge = lax.optimization_barrier((first, swapped_edge))
    result = call(
        column_last_kernel,
        [jax.ShapeDtypeStruct((levels, blocks, tokens, width), BF16)],
        [],
        [shifts, facts, anchor, resident_edge, normed_edge, gather(normed_edge, swapped_edge), first] + weights,
        10**9,
        [
            pltpu.VMEM((levels, tokens, width), BF16),
            pltpu.SMEM(shifts.shape, jnp.int32),
            pltpu.SemaphoreType.DMA((3,)),
        ],
        [pltpu.HBM] + [pltpu.VMEM] * (6 + len(weights)),
        out_spaces=[pltpu.HBM],
    )
    return result.reshape(fields.shape)


def solution(mesh):
    return jax.shard_map(
        local,
        mesh=mesh,
        in_specs=(P("lev", None, "lon", None), P(), P(), P(), P(), P(), P(), P(), P(), P()),
        out_specs=P("lev", None, "lon", None),
        check_vma=False,
    )
```

time: 153 us -> 48.8 us (0.32)
  waiting for transfers between devices: 37 us -> 0.18 us
  local copies, waits for them, and re-layouts: 32.7 us -> 0.03 us
  matrix products: 28.2 us -> 0 us
  Pallas kernels: 0 us -> 12.7 us
  other arithmetic: 10.6 us -> 0.1 us
  between operations: 8.03 us -> 0.17 us
  blocking collectives: 14.1 us -> 8 us
  starting transfers between devices: 21.5 us -> 27.3 us
    ppermute x2 -> x5, waiting for transfers between devices: 29 us -> 0.18 us  [the longest x1 0.17 us: local(): ahead_other = lax.ppermute(other, 'lon', west)]
    dot_general x11 -> x0, matrix products: 24.6 us -> none  [the longest x2 5.01 us: window_attend(): jnp.einsum('lnhqk,lnhkd->lnhqd', weights_bf, to_windows(values_in), prefe...]
    another operation x10 -> x0, local copies, waits for them, and re-layouts: 16.4 us -> none  [the longest x6 7.85 us: to_windows(): tensor.reshape(level_count, row_count, windows, WIN_LON, HEADS, head_size)]
    all_to_all x1 -> x0, blocking collectives: 14.1 us -> none  [local(): lax.all_to_all(resident, 'lev', split_axis=2, concat_axis=0, tiled=True)]
    pallas_call x0 -> x5, Pallas kernels: none -> 12.7 us  [call(): pl.pallas_call(body, out_shape=outs[0] if single else outs, in_specs=[pl....]
    ppermute x2 -> x5, starting transfers between devices: 17.1 us -> 27.3 us  [the longest x1 13 us: local(): ahead_other = lax.ppermute(other, 'lon', west)]
    all_to_all x1 -> x0, waiting for transfers between devices: 8 us -> none  [local(): lax.all_to_all(finished, 'lev', split_axis=0, concat_axis=2, tiled=True)]
    all_gather x0 -> x2, blocking collectives: none -> 8 us  [gather(): lax.all_gather(jnp.stack([part, other]), 'lev', tiled=True, axis_index_gr...]
  transfers between devices with their start and end apart: 3 -> 5, of which waited for: 3 -> 1; matrix products, arithmetic and copies ran while one was open for 2% -> 0% of each run, Pallas kernels for 0% -> 15%
where the time goes in v2:
time: 48.8 us; the launch traced here: 48.5 us
  starting transfers between devices  27.3 us (56%)
  Pallas kernels  12.7 us (26%)
  blocking collectives  8 us (16%)
    ppermute x1, starting transfers between devices, local(): ahead_other = lax.ppermute(other, 'lon', west)  13 us
    pallas_call x5, Pallas kernels, call(): pl.pallas_call(body, out_shape=outs[0] if single else outs, in_specs=[pl....  12.7 us
    all_gather x2, blocking collectives, gather(): lax.all_gather(jnp.stack([part, other]), 'lev', tiled=True, axis_index_gr...  8 us
    ppermute x2, starting transfers between devices, local(): lax.ppermute(part, 'lev', swap)  6.84 us
    ppermute x1, starting transfers between devices, local(): behind = lax.ppermute(sent, 'lon', [pair[::-1] for pair in west])  4.03 us
    ppermute x1, starting transfers between devices, local(): ahead_edge = lax.ppermute(edge, 'lon', west)  3.36 us
  transfers between devices with their start and end apart: 5, of which 1 were waited for; matrix products, arithmetic and copies ran while one was open for 0% of the time, Pallas kernels for 15%

profile of v2, /device:TPU:1, one launch (start us, length us, event | category | flops | bytes accessed | tf_op | source)
XLA Modules:
  0.0 48.5 jit_solution(17528025442114490654)
XLA Ops:
  0.0 1.4 %shard_map.100 = (bf16[17,16,384]{2,1,0:T(8,128)(2,1)S(1)}, bf16[16,16,384]{2,1,0:T(8,128)(2,1)S(1)}, bf16[16,16,384]{2,1,0:T(8,128)(2,1)S(1)}, s32[16,128]{1,0:...) custom-call(s32[2]{0:T(128)} %shifts_hbm.3, s32[8]{0:T(128)} %counts_hbm.1, ...), custom_call_target="tpu_custom_call" | custom-call | flops 1000000 | bytes 1577512 | tf_op jit(solution)/shard_map/pallas_call | solution.py:280
  1.4 4.0 %collective-permute-start = (bf16[17,16,384]{2,1,0:T(8,128)(2,1)S(1)}, bf16[17,16,384]{2,1,0:T(8,128)(2,1)S(1)}, u32[]{:S(2)}, u32[]{:S(2)}) collective-permute-start(bf16[17,16,384]{2,1,0:T(8,128)(2,1)S(1)} %get-tuple-element.20), channel_id=1, source_target_pairs={{508,0},{0,4},{4,8},{8,12},{12,16},{16,20},{20,24},{24,28},{28,32}... | collective-permute-start | bytes 626696 | tf_op jit(solution)/shard_map/ppermute | solution.py:335
  5.5 13.0 %collective-permute-start.2 = (bf16[16,16,384]{2,1,0:T(8,128)(2,1)S(1)}, bf16[16,16,384]{2,1,0:T(8,128)(2,1)S(1)}, u32[]{:S(2)}, u32[]{:S(2)}) collective-permute-start(bf16[16,16,384]{2,1,0:T(8,128)(2,1)S(1)} %get-tuple-element.24.own_ref), channel_id=1, source_target_pairs={{0,508},{4,0},{8,4},{12,8},{16,12},{20,16},{24,20},{28,24},{32,28}... | collective-permute-start | bytes 589832 | tf_op jit(solution)/shard_map/ppermute | solution.py:336
  18.5 3.4 %collective-permute-start.1 = (bf16[16,16,384]{2,1,0:T(8,128)(2,1)S(1)}, bf16[16,16,384]{2,1,0:T(8,128)(2,1)S(1)}, u32[]{:S(2)}, u32[]{:S(2)}) collective-permute-start(bf16[16,16,384]{2,1,0:T(8,128)(2,1)S(1)} %get-tuple-element.19.own_ref), channel_id=1, source_target_pairs={{0,508},{4,0},{8,4},{12,8},{16,12},{20,16},{24,20},{28,24},{32,28}... | collective-permute-start | bytes 589832 | tf_op jit(solution)/shard_map/ppermute | solution.py:339
  21.9 0.2 collective-permute-done.2.ahead_ref
  22.1 0.0 collective-permute-done.behind_ref
  22.1 2.1 %shard_map.101 = (bf16[256,384]{1,0:T(8,128)(2,1)S(1)}, bf16[256,384]{1,0:T(8,128)(2,1)S(1)}) custom-call(s32[16,128]{1,0:T(8,128)S(1)} %get-tuple-element.18.facts_ref, s32[8,128]{1,0:T(8,128)S(1)} %broadcast_in_dim.3.anchor_ref, bf16[16,16,384]{2,1,0:T(8,128)(2,1)S(1)} %get-tuple-element.24.own_ref, ...), custom_call_target="tpu_custom_call" | custom-call | flops 1000000000 | bytes 1798656 | tf_op jit(solution)/shard_map/pallas_call | solution.py:280
  24.2 4.5 %collective-permute-start.3 = (bf16[256,384]{1,0:T(8,128)(2,1)S(1)}, bf16[256,384]{1,0:T(8,128)(2,1)S(1)}, u32[]{:S(2)}, u32[]{:S(2)}) collective-permute-start(bf16[256,384]{1,0:T(8,128)(2,1)S(1)} %get-tuple-element.28.normed_ref), channel_id=1, source_target_pairs={{0,2},{1,3},{2,0},{3,1},{4,6},{5,7},{6,4},{7,5},{8,10},{9,11},{10,... | collective-permute-start | bytes 589832 | tf_op jit(solution)/shard_map/ppermute | solution.py:363
  28.7 0.0 collective-permute-done.1.ahead_ref
  28.7 0.0 copy-start.2
  28.7 2.1 %shard_map.102 = (bf16[256,384]{1,0:T(8,128)(2,1)S(1)}, bf16[256,384]{1,0:T(8,128)(2,1)S(1)}) custom-call(s32[16,128]{1,0:T(8,128)S(1)} %get-tuple-element.18.facts_ref, s32[8,128]{1,0:T(8,128)S(1)} %broadcast_in_dim.3.anchor_ref, bf16[16,16,384]{2,1,0:T(8,128)(2,1)S(1)} %get-tuple-element.19.own_ref, ...), custom_call_target="tpu_custom_call" | custom-call | flops 1000000000 | bytes 1995264 | tf_op jit(solution)/shard_map/pallas_call | solution.py:280
  30.8 2.3 %collective-permute-start.4 = (bf16[256,384]{1,0:T(8,128)(2,1)S(1)}, bf16[256,384]{1,0:T(8,128)(2,1)S(1)}, u32[]{:S(2)}, u32[]{:S(2)}) collective-permute-start(bf16[256,384]{1,0:T(8,128)(2,1)S(1)} %get-tuple-element.27.normed_ref), channel_id=1, source_target_pairs={{0,2},{1,3},{2,0},{3,1},{4,6},{5,7},{6,4},{7,5},{8,10},{9,11},{10,... | collective-permute-start | bytes 589832 | tf_op jit(solution)/shard_map/ppermute | solution.py:363
  33.1 0.0 collective-permute-done.3
  33.1 0.0 copy-start
  33.2 0.0 copy-start.1
  33.2 0.0 copy-start.3
  33.2 0.0 copy-start.4
  33.2 4.9 %all_gather.6.gathered_ref = bf16[4,256,384]{2,1,0:T(8,128)(2,1)S(1)} all-gather(bf16[2,256,384]{2,1,0:T(8,128)(2,1)S(1)} %pad_maximum_fusion), channel_id=1, replica_groups={{0,1},{2,3},{4,5},{6,7},{8,9},{10,11},{12,13},{14,15},{16,17},{18,19},{..., dimensions={0}, use_global_device_ids=true | all-gather | bytes 1179648 | tf_op jit(solution)/shard_map/all_gather | solution.py:361
  38.2 0.0 copy-done.2
  38.2 0.0 copy-done
  38.2 0.0 copy-done.1
  38.2 0.0 copy-done.3
  38.2 0.0 copy-done.4
  38.2 3.2 %shard_map.103.first_ref = bf16[4,64,384]{2,1,0:T(8,128)(2,1)S(1)} custom-call(s32[16,128]{1,0:T(8,128)S(1)} %get-tuple-element.18.facts_ref, s32[8,128]{1,0:T(8,128)S(1)} %broadcast_in_dim.3.anchor_ref, bf16[256,384]{1,0:T(8,128)(2,1)S(1)} %get-tuple-element.25._.resident_ref, bf16[256,384]{1,0:T(8,128)(2,1)S(1)} %get-tuple-element.28.normed_ref, ...), custom_call_target="tpu_custom_call" | custom-call | flops 1000000000 | bytes 3555840 | tf_op jit(solution)/shard_map/pallas_call | solution.py:280
  41.4 0.0 collective-permute-done.4
  41.5 3.1 %all_gather.7.gathered_ref = bf16[4,256,384]{2,1,0:T(8,128)(2,1)S(1)} all-gather(bf16[2,256,384]{2,1,0:T(8,128)(2,1)S(1)} %pad_maximum_fusion.1), channel_id=1, replica_groups={{0,1},{2,3},{4,5},{6,7},{8,9},{10,11},{12,13},{14,15},{16,17},{18,19},{..., dimensions={0}, use_global_device_ids=true | all-gather | bytes 1179648 | tf_op jit(solution)/shard_map/all_gather | solution.py:361
  44.5 4.0 %shard_map.104 = bf16[4,2,64,384]{3,2,1,0:T(8,128)(2,1)} custom-call(s32[2]{0:T(128)} %shifts_hbm.3, s32[16,128]{1,0:T(8,128)S(1)} %get-tuple-element.18.facts_ref, s32[8,128]{1,0:T(8,128)S(1)} %broadcast_in_dim.3.anchor_ref, bf16[256,384]{1,0:T(8,128)(2,1)S(1)} %get-tuple-element.26.resident_ref, bf16[256,384]{1,0:T(8,128)(2,1)S(1)} %get-tuple-element.27.normed_ref, ...), custom_call_target="tpu_custom_call" | custom-call | flops 1000000000 | bytes 3752456 | tf_op jit(solution)/shard_map/pallas_call | solution.py:280
  (3 shorter events, 0.1 us)
Async XLA Ops:
  1.4 20.6 %collective-permute-start = (bf16[17,16,384]{2,1,0:T(8,128)(2,1)S(1)}, bf16[17,16,384]{2,1,0:T(8,128)(2,1)S(1)}, u32[]{:S(2)}, u32[]{:S(2)}) collective-permute-start(bf16[17,16,384]{2,1,0:T(8,128)(2,1)S(1)} %get-tuple-element.20), channel_id=1, source_target_pairs={{508,0},{0,4},{4,8},{8,12},{12,16},{16,20},{20,24},{24,28},{28,32}... | collective-permute-start | bytes 626696 | tf_op jit(solution)/shard_map/ppermute | solution.py:335
  5.5 16.6 %collective-permute-start.2 = (bf16[16,16,384]{2,1,0:T(8,128)(2,1)S(1)}, bf16[16,16,384]{2,1,0:T(8,128)(2,1)S(1)}, u32[]{:S(2)}, u32[]{:S(2)}) collective-permute-start(bf16[16,16,384]{2,1,0:T(8,128)(2,1)S(1)} %get-tuple-element.24.own_ref), channel_id=1, source_target_pairs={{0,508},{4,0},{8,4},{12,8},{16,12},{20,16},{24,20},{28,24},{32,28}... | collective-permute-start | bytes 589832 | tf_op jit(solution)/shard_map/ppermute | solution.py:336
  18.5 10.2 %collective-permute-start.1 = (bf16[16,16,384]{2,1,0:T(8,128)(2,1)S(1)}, bf16[16,16,384]{2,1,0:T(8,128)(2,1)S(1)}, u32[]{:S(2)}, u32[]{:S(2)}) collective-permute-start(bf16[16,16,384]{2,1,0:T(8,128)(2,1)S(1)} %get-tuple-element.19.own_ref), channel_id=1, source_target_pairs={{0,508},{4,0},{8,4},{12,8},{16,12},{20,16},{24,20},{28,24},{32,28}... | collective-permute-start | bytes 589832 | tf_op jit(solution)/shard_map/ppermute | solution.py:339
  24.2 9.0 %collective-permute-start.3 = (bf16[256,384]{1,0:T(8,128)(2,1)S(1)}, bf16[256,384]{1,0:T(8,128)(2,1)S(1)}, u32[]{:S(2)}, u32[]{:S(2)}) collective-permute-start(bf16[256,384]{1,0:T(8,128)(2,1)S(1)} %get-tuple-element.28.normed_ref), channel_id=1, source_target_pairs={{0,2},{1,3},{2,0},{3,1},{4,6},{5,7},{6,4},{7,5},{8,10},{9,11},{10,... | collective-permute-start | bytes 589832 | tf_op jit(solution)/shard_map/ppermute | solution.py:363
  28.7 9.5 %copy-start.2 = (bf16[768,384]{1,0:T(8,128)(2,1)S(1)}, bf16[768,384]{1,0:T(8,128)(2,1)}, u32[]{:S(2)}) copy-start(bf16[768,384]{1,0:T(8,128)(2,1)} %mlp_ref.3) | copy-start | bytes 1769476
  30.8 10.6 %collective-permute-start.4 = (bf16[256,384]{1,0:T(8,128)(2,1)S(1)}, bf16[256,384]{1,0:T(8,128)(2,1)S(1)}, u32[]{:S(2)}, u32[]{:S(2)}) collective-permute-start(bf16[256,384]{1,0:T(8,128)(2,1)S(1)} %get-tuple-element.27.normed_ref), channel_id=1, source_target_pairs={{0,2},{1,3},{2,0},{3,1},{4,6},{5,7},{6,4},{7,5},{8,10},{9,11},{10,... | collective-permute-start | bytes 589832 | tf_op jit(solution)/shard_map/ppermute | solution.py:363
  33.1 5.1 %copy-start = (bf16[3,384,384]{2,1,0:T(8,128)(2,1)S(1)}, bf16[3,384,384]{2,1,0:T(8,128)(2,1)}, u32[]{:S(2)}) copy-start(bf16[3,384,384]{2,1,0:T(8,128)(2,1)} %qkv_ref.3) | copy-start | bytes 2654212
  33.2 5.0 %copy-start.1 = (bf16[384,768]{1,0:T(8,128)(2,1)S(1)}, bf16[384,768]{1,0:T(8,128)(2,1)}, u32[]{:S(2)}) copy-start(bf16[384,768]{1,0:T(8,128)(2,1)} %in_ref.3) | copy-start | bytes 1769476
  33.2 5.0 %copy-start.3 = (bf16[384,384]{1,0:T(8,128)(2,1)S(1)}, bf16[384,384]{1,0:T(8,128)(2,1)}, u32[]{:S(2)}) copy-start(bf16[384,384]{1,0:T(8,128)(2,1)} %out_w_ref.3) | copy-start | bytes 884740
  33.2 5.0 %copy-start.4 = (f32[3,384]{1,0:T(4,128)S(1)}, f32[3,384]{1,0:T(4,128)}, u32[]{:S(2)}) copy-start(f32[3,384]{1,0:T(4,128)} %gains_ref.3) | copy-start | bytes 13828

commit v3 on v2

--- a/solution.py
+++ b/solution.py
@@ -118,18 +118,25 @@
         copy.wait()
 
 
+def own_kernel(edge_ref, other_ref, gains_ref, qkv_ref, edge_out_ref, other_out_ref):
+    total, width = edge_out_ref.shape[1:]
+    outs = (edge_out_ref, other_out_ref)
+    normed = [
+        layer_norm(own[...].reshape(total, width).astype(F32), gains_ref[0:1]) for own in (edge_ref, other_ref)
+    ]
+    for n in range(3):
+        for part, out_ref in zip(normed, outs):
+            out_ref[n] = dot32(part, qkv_ref[n]).astype(BF16)
+
+
 def window_block(
-    circle, shift, counts_row, other, own, facts_ref, anchor_ref, gains_ref, qkv_ref, out_w_ref, result_ref, normed_ref
+    circle, shift, counts_row, other, own, done_ref, facts_ref, anchor_ref, gains_ref, qkv_ref, out_w_ref, result_ref,
+    normed_ref,
 ):
     total, width = own.shape
     tokens = WIN_ROWS * WIN_LON
     anchor = anchor_ref[:1, :1]
-    normed = layer_norm(own, gains_ref[0:1])
-    queries = dot32(normed, qkv_ref[0]).astype(BF16)
-    other = layer_norm(other, gains_ref[0:1])
-    normed = jnp.concatenate(
-        [part[first : first + tokens] for first in range(0, total, tokens) for part in (normed, other)], axis=0
-    )
+    normed = layer_norm(other, gains_ref[0:1])
     keys, values = [dot32(normed, qkv_ref[n]).astype(BF16) for n in (1, 2)]
 
     shape = (tokens, 2 * tokens)
@@ -144,8 +151,14 @@
     allowed = (here == same) & (cell < count_of_row(facts_ref, counts_row, (key // WIN_LON) % WIN_ROWS))
     units = []
     for first in range(0, total, tokens):
-        both = slice(2 * first, 2 * (first + tokens))
-        units.append((queries[first : first + tokens], keys[both], values[both]))
+        at = slice(first, first + tokens)
+        units.append(
+            (
+                done_ref[0, at],
+                jnp.concatenate([done_ref[1, at], keys[at]], axis=0),
+                jnp.concatenate([done_ref[2, at], values[at]], axis=0),
+            )
+        )
     mixed = attend(units, allowed, width // HEADS)
     resident = (own + dot32(jnp.concatenate(mixed, axis=0), out_w_ref[...])).astype(BF16)
     result_ref[...] = resident
@@ -153,7 +166,7 @@
 
 
 def window_edge_kernel(
-    circle, facts_ref, anchor_ref, own_ref, behind_ref, ahead_ref, gains_ref, qkv_ref, out_w_ref, _,
+    circle, facts_ref, anchor_ref, own_ref, done_ref, behind_ref, ahead_ref, gains_ref, qkv_ref, out_w_ref, _,
     result_ref, normed_ref,
 ):
     total, width = result_ref.shape
@@ -164,13 +177,13 @@
     place = lax.broadcasted_iota(jnp.int32, (total, width), 0) % WIN_LON
     other = jnp.where(place == WIN_LON - 1, behind, ahead_ref[...].reshape(total, width).astype(F32))
     window_block(
-        circle, WIN_LON - 1, EDGE_COUNTS, other, own_ref[...].reshape(total, width).astype(F32), facts_ref,
+        circle, WIN_LON - 1, EDGE_COUNTS, other, own_ref[...].reshape(total, width).astype(F32), done_ref, facts_ref,
         anchor_ref, gains_ref, qkv_ref, out_w_ref, result_ref, normed_ref,
     )
 
 
 def window_both_kernel(
-    circle, facts_ref, anchor_ref, own_ref, behind_ref, ahead_ref, gains_ref, qkv_ref, out_w_ref, result_ref,
+    circle, facts_ref, anchor_ref, own_ref, done_ref, behind_ref, ahead_ref, gains_ref, qkv_ref, out_w_ref, result_ref,
     normed_ref,
 ):
     total, width = result_ref.shape
@@ -180,7 +193,7 @@
     ahead = ahead_ref[...].reshape(total, width).astype(F32)
     window_block(
         circle, shift, BOTH_COUNTS, jnp.where(place < shift, ahead, behind),
-        own_ref[...].reshape(total, width).astype(F32), facts_ref, anchor_ref, gains_ref, qkv_ref, out_w_ref,
+        own_ref[...].reshape(total, width).astype(F32), done_ref, facts_ref, anchor_ref, gains_ref, qkv_ref, out_w_ref,
         result_ref, normed_ref,
     )
 
@@ -336,22 +349,23 @@
     ahead_other = lax.ppermute(other, "lon", west)
 
     one = jax.ShapeDtypeStruct((total, width), BF16)
+    three = jax.ShapeDtypeStruct((3, total, width), BF16)
+    done_edge, done_other = call(own_kernel, [three, three], [], [edge, other] + weights[:2], 10**9)
     ahead_edge = lax.ppermute(edge, "lon", west)
-
     resident_other, normed_other = call(
         functools.partial(window_both_kernel, circle),
         [one, one],
         [],
-        [facts, anchor, other, behind, ahead_other] + weights,
+        [facts, anchor, other, done_other, behind, ahead_other] + weights,
         10**9,
     )
     resident_edge, normed_edge = call(
         functools.partial(window_edge_kernel, circle),
         [one, one],
         [],
-        [facts, anchor, edge, behind, ahead_edge] + weights + [resident_other],
+        [facts, anchor, edge, done_edge, behind, ahead_edge] + weights + [resident_other],
         10**9,
-        spaces=[pltpu.VMEM] * (5 + len(weights)) + [pl.ANY],
+        spaces=[pltpu.VMEM] * (6 + len(weights)) + [pl.ANY],
     )
 
     groups = [[first, first + 1] for first in range(0, 2 * CORES, CORES)]

time: 48.8 us -> 48.1 us (0.986)
  blocking collectives: 8 us -> 7.26 us
    all_gather x2, blocking collectives: 8 us -> 7.26 us  [gather(): lax.all_gather(jnp.stack([part, other]), 'lev', tiled=True, axis_index_gr...]
    pallas_call x5 -> x6, Pallas kernels: 12.7 us -> 13 us  [call(): pl.pallas_call(body, out_shape=outs[0] if single else outs, in_specs=[pl....]
  transfers between devices with their start and end apart: 5 -> 5, of which waited for: 1 -> 0; matrix products, arithmetic and copies ran while one was open for 0% -> 0% of each run, Pallas kernels for 15% -> 16%
where the time goes in v3:
time: 48.1 us; the launch traced here: 47.8 us
  starting transfers between devices  27.2 us (57%)
  Pallas kernels  13 us (27%)
  blocking collectives  7.26 us (15%)
    ppermute x1, starting transfers between devices, local(): ahead_other = lax.ppermute(other, 'lon', west)  13 us
    pallas_call x6, Pallas kernels, call(): pl.pallas_call(body, out_shape=outs[0] if single else outs, in_specs=[pl....  13 us
    all_gather x2, blocking collectives, gather(): lax.all_gather(jnp.stack([part, other]), 'lev', tiled=True, axis_index_gr...  7.26 us
    ppermute x2, starting transfers between devices, local(): lax.ppermute(part, 'lev', swap)  6.79 us
    ppermute x1, starting transfers between devices, local(): behind = lax.ppermute(sent, 'lon', [pair[::-1] for pair in west])  4.03 us
    ppermute x1, starting transfers between devices, local(): ahead_edge = lax.ppermute(edge, 'lon', west)  3.36 us
  transfers between devices with their start and end apart: 5, of which 0 were waited for; matrix products, arithmetic and copies ran while one was open for 0% of the time, Pallas kernels for 16%

profile of v3, /device:TPU:1, one launch (start us, length us, event | category | flops | bytes accessed | tf_op | source)
XLA Modules:
  0.0 47.8 jit_solution(11109001780464130103)
XLA Ops:
  0.0 1.4 %shard_map.100 = (bf16[17,16,384]{2,1,0:T(8,128)(2,1)S(1)}, bf16[16,16,384]{2,1,0:T(8,128)(2,1)S(1)}, bf16[16,16,384]{2,1,0:T(8,128)(2,1)S(1)}, s32[16,128]{1,0:...) custom-call(s32[2]{0:T(128)} %shifts_hbm.3, s32[8]{0:T(128)} %counts_hbm.1, ...), custom_call_target="tpu_custom_call" | custom-call | flops 1000000 | bytes 1577512 | tf_op jit(solution)/shard_map/pallas_call | solution.py:293
  1.4 4.0 %collective-permute-start = (bf16[17,16,384]{2,1,0:T(8,128)(2,1)S(1)}, bf16[17,16,384]{2,1,0:T(8,128)(2,1)S(1)}, u32[]{:S(2)}, u32[]{:S(2)}) collective-permute-start(bf16[17,16,384]{2,1,0:T(8,128)(2,1)S(1)} %get-tuple-element.26), channel_id=1, source_target_pairs={{508,0},{0,4},{4,8},{8,12},{12,16},{16,20},{20,24},{24,28},{28,32}... | collective-permute-start | bytes 626696 | tf_op jit(solution)/shard_map/ppermute | solution.py:348
  5.5 13.0 %collective-permute-start.2 = (bf16[16,16,384]{2,1,0:T(8,128)(2,1)S(1)}, bf16[16,16,384]{2,1,0:T(8,128)(2,1)S(1)}, u32[]{:S(2)}, u32[]{:S(2)}) collective-permute-start(bf16[16,16,384]{2,1,0:T(8,128)(2,1)S(1)} %get-tuple-element.22.other_ref.own_ref), channel_id=1, source_target_pairs={{0,508},{4,0},{8,4},{12,8},{16,12},{20,16},{24,20},{28,24},{32,28}... | collective-permute-start | bytes 589832 | tf_op jit(solution)/shard_map/ppermute | solution.py:349
  18.5 3.4 %collective-permute-start.1 = (bf16[16,16,384]{2,1,0:T(8,128)(2,1)S(1)}, bf16[16,16,384]{2,1,0:T(8,128)(2,1)S(1)}, u32[]{:S(2)}, u32[]{:S(2)}) collective-permute-start(bf16[16,16,384]{2,1,0:T(8,128)(2,1)S(1)} %get-tuple-element.21.edge_ref.own_ref), channel_id=1, source_target_pairs={{0,508},{4,0},{8,4},{12,8},{16,12},{20,16},{24,20},{28,24},{32,28}... | collective-permute-start | bytes 589832 | tf_op jit(solution)/shard_map/ppermute | solution.py:354
  21.9 1.2 %shard_map.101 = (bf16[3,256,384]{2,1,0:T(8,128)(2,1)S(1)}, bf16[3,256,384]{2,1,0:T(8,128)(2,1)S(1)}) custom-call(bf16[16,16,384]{2,1,0:T(8,128)(2,1)S(1)} %get-tuple-element.21.edge_ref.own_ref, bf16[16,16,384]{2,1,0:T(8,128)(2,1)S(1)} %get-tuple-element.22.other_ref.own_ref, f32[3,384]{1,0:T(4,128)S(1)} %get-tuple-element.23.gains_ref, ...), custom_call_target="tpu_custom_call" | custom-call | flops 1000000000 | bytes 1282560 | tf_op jit(solution)/shard_map/pallas_call | solution.py:293
  23.1 0.0 collective-permute-done.2.ahead_ref
  23.1 0.0 collective-permute-done.behind_ref
  23.1 1.6 %shard_map.102 = (bf16[256,384]{1,0:T(8,128)(2,1)S(1)}, bf16[256,384]{1,0:T(8,128)(2,1)S(1)}) custom-call(s32[16,128]{1,0:T(8,128)S(1)} %get-tuple-element.20.facts_ref, s32[8,128]{1,0:T(8,128)S(1)} %broadcast_in_dim.3.anchor_ref, bf16[16,16,384]{2,1,0:T(8,128)(2,1)S(1)} %get-tuple-element.22.other_ref.own_ref, ...), custom_call_target="tpu_custom_call" | custom-call | flops 1000000000 | bytes 2388480 | tf_op jit(solution)/shard_map/pallas_call | solution.py:293
  24.8 4.5 %collective-permute-start.3 = (bf16[256,384]{1,0:T(8,128)(2,1)S(1)}, bf16[256,384]{1,0:T(8,128)(2,1)S(1)}, u32[]{:S(2)}, u32[]{:S(2)}) collective-permute-start(bf16[256,384]{1,0:T(8,128)(2,1)S(1)} %get-tuple-element.32.normed_ref), channel_id=1, source_target_pairs={{0,2},{1,3},{2,0},{3,1},{4,6},{5,7},{6,4},{7,5},{8,10},{9,11},{10,... | collective-permute-start | bytes 589832 | tf_op jit(solution)/shard_map/ppermute | solution.py:377
  29.3 0.0 collective-permute-done.1.ahead_ref
  29.3 0.0 copy-start.2
  29.3 1.6 %shard_map.103 = (bf16[256,384]{1,0:T(8,128)(2,1)S(1)}, bf16[256,384]{1,0:T(8,128)(2,1)S(1)}) custom-call(s32[16,128]{1,0:T(8,128)S(1)} %get-tuple-element.20.facts_ref, s32[8,128]{1,0:T(8,128)S(1)} %broadcast_in_dim.3.anchor_ref, bf16[16,16,384]{2,1,0:T(8,128)(2,1)S(1)} %get-tuple-element.21.edge_ref.own_ref, ...), custom_call_target="tpu_custom_call" | custom-call | flops 1000000000 | bytes 2585088 | tf_op jit(solution)/shard_map/pallas_call | solution.py:293
  30.9 2.3 %collective-permute-start.4 = (bf16[256,384]{1,0:T(8,128)(2,1)S(1)}, bf16[256,384]{1,0:T(8,128)(2,1)S(1)}, u32[]{:S(2)}, u32[]{:S(2)}) collective-permute-start(bf16[256,384]{1,0:T(8,128)(2,1)S(1)} %get-tuple-element.31.normed_ref), channel_id=1, source_target_pairs={{0,2},{1,3},{2,0},{3,1},{4,6},{5,7},{6,4},{7,5},{8,10},{9,11},{10,... | collective-permute-start | bytes 589832 | tf_op jit(solution)/shard_map/ppermute | solution.py:377
  33.2 0.0 collective-permute-done.3
  33.2 0.0 copy-start
  33.3 0.0 copy-start.1
  33.3 0.0 copy-start.3
  33.3 0.0 copy-start.4
  33.3 4.4 %all_gather.6.gathered_ref = bf16[4,256,384]{2,1,0:T(8,128)(2,1)S(1)} all-gather(bf16[2,256,384]{2,1,0:T(8,128)(2,1)S(1)} %pad_maximum_fusion), channel_id=1, replica_groups={{0,1},{2,3},{4,5},{6,7},{8,9},{10,11},{12,13},{14,15},{16,17},{18,19},{..., dimensions={0}, use_global_device_ids=true | all-gather | bytes 1179648 | tf_op jit(solution)/shard_map/all_gather | solution.py:375
  37.7 0.0 copy-done.2
  37.7 0.0 copy-done
  37.7 0.0 copy-done.1
  37.7 0.0 copy-done.3
  37.7 0.0 copy-done.4
  37.7 3.2 %shard_map.104.first_ref = bf16[4,64,384]{2,1,0:T(8,128)(2,1)S(1)} custom-call(s32[16,128]{1,0:T(8,128)S(1)} %get-tuple-element.20.facts_ref, s32[8,128]{1,0:T(8,128)S(1)} %broadcast_in_dim.3.anchor_ref, bf16[256,384]{1,0:T(8,128)(2,1)S(1)} %get-tuple-element.29._.resident_ref, bf16[256,384]{1,0:T(8,128)(2,1)S(1)} %get-tuple-element.32.normed_ref, ...), custom_call_target="tpu_custom_call" | custom-call | flops 1000000000 | bytes 3555840 | tf_op jit(solution)/shard_map/pallas_call | solution.py:293
  40.9 0.0 collective-permute-done.4
  41.0 2.9 %all_gather.7.gathered_ref = bf16[4,256,384]{2,1,0:T(8,128)(2,1)S(1)} all-gather(bf16[2,256,384]{2,1,0:T(8,128)(2,1)S(1)} %pad_maximum_fusion.1), channel_id=1, replica_groups={{0,1},{2,3},{4,5},{6,7},{8,9},{10,11},{12,13},{14,15},{16,17},{18,19},{..., dimensions={0}, use_global_device_ids=true | all-gather | bytes 1179648 | tf_op jit(solution)/shard_map/all_gather | solution.py:375
  43.9 4.0 %shard_map.105 = bf16[4,2,64,384]{3,2,1,0:T(8,128)(2,1)} custom-call(s32[2]{0:T(128)} %shifts_hbm.3, s32[16,128]{1,0:T(8,128)S(1)} %get-tuple-element.20.facts_ref, s32[8,128]{1,0:T(8,128)S(1)} %broadcast_in_dim.3.anchor_ref, bf16[256,384]{1,0:T(8,128)(2,1)S(1)} %get-tuple-element.30.resident_ref, bf16[256,384]{1,0:T(8,128)(2,1)S(1)} %get-tuple-element.31.normed_ref, ...), custom_call_target="tpu_custom_call" | custom-call | flops 1000000000 | bytes 3752456 | tf_op jit(solution)/shard_map/pallas_call | solution.py:293
  (3 shorter events, 0.1 us)
Async XLA Ops:
  1.4 21.7 %collective-permute-start = (bf16[17,16,384]{2,1,0:T(8,128)(2,1)S(1)}, bf16[17,16,384]{2,1,0:T(8,128)(2,1)S(1)}, u32[]{:S(2)}, u32[]{:S(2)}) collective-permute-start(bf16[17,16,384]{2,1,0:T(8,128)(2,1)S(1)} %get-tuple-element.26), channel_id=1, source_target_pairs={{508,0},{0,4},{4,8},{8,12},{12,16},{16,20},{20,24},{24,28},{28,32}... | collective-permute-start | bytes 626696 | tf_op jit(solution)/shard_map/ppermute | solution.py:348
  5.5 17.6 %collective-permute-start.2 = (bf16[16,16,384]{2,1,0:T(8,128)(2,1)S(1)}, bf16[16,16,384]{2,1,0:T(8,128)(2,1)S(1)}, u32[]{:S(2)}, u32[]{:S(2)}) collective-permute-start(bf16[16,16,384]{2,1,0:T(8,128)(2,1)S(1)} %get-tuple-element.22.other_ref.own_ref), channel_id=1, source_target_pairs={{0,508},{4,0},{8,4},{12,8},{16,12},{20,16},{24,20},{28,24},{32,28}... | collective-permute-start | bytes 589832 | tf_op jit(solution)/shard_map/ppermute | solution.py:349
  18.5 10.8 %collective-permute-start.1 = (bf16[16,16,384]{2,1,0:T(8,128)(2,1)S(1)}, bf16[16,16,384]{2,1,0:T(8,128)(2,1)S(1)}, u32[]{:S(2)}, u32[]{:S(2)}) collective-permute-start(bf16[16,16,384]{2,1,0:T(8,128)(2,1)S(1)} %get-tuple-element.21.edge_ref.own_ref), channel_id=1, source_target_pairs={{0,508},{4,0},{8,4},{12,8},{16,12},{20,16},{24,20},{28,24},{32,28}... | collective-permute-start | bytes 589832 | tf_op jit(solution)/shard_map/ppermute | solution.py:354
  24.8 8.5 %collective-permute-start.3 = (bf16[256,384]{1,0:T(8,128)(2,1)S(1)}, bf16[256,384]{1,0:T(8,128)(2,1)S(1)}, u32[]{:S(2)}, u32[]{:S(2)}) collective-permute-start(bf16[256,384]{1,0:T(8,128)(2,1)S(1)} %get-tuple-element.32.normed_ref), channel_id=1, source_target_pairs={{0,2},{1,3},{2,0},{3,1},{4,6},{5,7},{6,4},{7,5},{8,10},{9,11},{10,... | collective-permute-start | bytes 589832 | tf_op jit(solution)/shard_map/ppermute | solution.py:377
  29.3 8.4 %copy-start.2 = (bf16[768,384]{1,0:T(8,128)(2,1)S(1)}, bf16[768,384]{1,0:T(8,128)(2,1)}, u32[]{:S(2)}) copy-start(bf16[768,384]{1,0:T(8,128)(2,1)} %mlp_ref.3) | copy-start | bytes 1769476
  30.9 10.0 %collective-permute-start.4 = (bf16[256,384]{1,0:T(8,128)(2,1)S(1)}, bf16[256,384]{1,0:T(8,128)(2,1)S(1)}, u32[]{:S(2)}, u32[]{:S(2)}) collective-permute-start(bf16[256,384]{1,0:T(8,128)(2,1)S(1)} %get-tuple-element.31.normed_ref), channel_id=1, source_target_pairs={{0,2},{1,3},{2,0},{3,1},{4,6},{5,7},{6,4},{7,5},{8,10},{9,11},{10,... | collective-permute-start | bytes 589832 | tf_op jit(solution)/shard_map/ppermute | solution.py:377
  33.2 4.5 %copy-start = (bf16[3,384,384]{2,1,0:T(8,128)(2,1)S(1)}, bf16[3,384,384]{2,1,0:T(8,128)(2,1)}, u32[]{:S(2)}) copy-start(bf16[3,384,384]{2,1,0:T(8,128)(2,1)} %qkv_ref.3) | copy-start | bytes 2654212
  33.3 4.4 %copy-start.1 = (bf16[384,768]{1,0:T(8,128)(2,1)S(1)}, bf16[384,768]{1,0:T(8,128)(2,1)}, u32[]{:S(2)}) copy-start(bf16[384,768]{1,0:T(8,128)(2,1)} %in_ref.3) | copy-start | bytes 1769476
  33.3 4.4 %copy-start.3 = (bf16[384,384]{1,0:T(8,128)(2,1)S(1)}, bf16[384,384]{1,0:T(8,128)(2,1)}, u32[]{:S(2)}) copy-start(bf16[384,384]{1,0:T(8,128)(2,1)} %out_w_ref.3) | copy-start | bytes 884740
  33.3 4.4 %copy-start.4 = (f32[3,384]{1,0:T(4,128)S(1)}, f32[3,384]{1,0:T(4,128)}, u32[]{:S(2)}) copy-start(f32[3,384]{1,0:T(4,128)} %gains_ref.3) | copy-start | bytes 13828

commit v4 on v3

--- a/solution.py
+++ b/solution.py
@@ -86,18 +86,15 @@
 
 
 def pack_kernel(
-    shifts_hbm, counts_hbm, fields_hbm, gains_hbm, qkv_hbm, out_w_hbm, east_ref, edge_ref, other_ref, facts_ref,
-    gains_ref, qkv_ref, out_w_ref, shifts_ref, counts_ref, fields_ref, sems,
+    shifts_hbm, counts_hbm, fields_hbm, east_ref, edge_ref, other_ref, facts_ref, shifts_ref, counts_ref, fields_ref,
+    sems,
 ):
     runs, cells, width = edge_ref.shape
-    moves = [
-        (shifts_hbm, shifts_ref), (counts_hbm, counts_ref), (fields_hbm, fields_ref), (gains_hbm, gains_ref),
-        (qkv_hbm, qkv_ref), (out_w_hbm, out_w_ref),
-    ]
+    moves = [(shifts_hbm, shifts_ref), (counts_hbm, counts_ref), (fields_hbm, fields_ref)]
     copies = [pltpu.make_async_copy(*ends, sems.at[n]) for n, ends in enumerate(moves)]
     for copy in copies:
         copy.start()
-    for copy in copies[:3]:
+    for copy in copies:
         copy.wait()
     block = edge_block(shifts_ref)
     edge = fields_ref[:, block].reshape(runs, cells, width)
@@ -114,8 +111,6 @@
     for row, number in enumerate(numbers):
         facts = jnp.where(place == row, number, facts)
     facts_ref[...] = facts
-    for copy in copies[3:]:
-        copy.wait()
 
 
 def own_kernel(edge_ref, other_ref, gains_ref, qkv_ref, edge_out_ref, other_out_ref):
@@ -324,25 +319,24 @@
     anchor = jnp.full((8, LANES), lax.axis_index("lon") * cells, jnp.int32)
 
     weights = [norm_gains, window_qkv, window_out]
-    sent, edge, other, facts, *weights = call(
+    sent, edge, other, facts = call(
         pack_kernel,
         [
             jax.ShapeDtypeStruct((1 + runs, cells, width), BF16),
             jax.ShapeDtypeStruct((runs, cells, width), BF16),
             jax.ShapeDtypeStruct((runs, cells, width), BF16),
             jax.ShapeDtypeStruct((FACTS, LANES), jnp.int32),
-        ]
-        + [jax.ShapeDtypeStruct(array.shape, array.dtype) for array in weights],
+        ],
         [],
-        [shifts, counts, fields.reshape(levels, blocks, WIN_ROWS, cells, width)] + weights,
-        10**6,
+        [shifts, counts, fields.reshape(levels, blocks, WIN_ROWS, cells, width)],
+        10**10,
         [
             pltpu.SMEM(shifts.shape, jnp.int32),
             pltpu.SMEM(counts.shape, jnp.int32),
             pltpu.VMEM((levels, blocks, WIN_ROWS, cells, width), BF16),
             pltpu.SemaphoreType.DMA((6,)),
         ],
-        [pltpu.HBM] * 6,
+        [pltpu.HBM] * 3,
     )
     west = [(tile, (tile - 1) % tiles) for tile in range(tiles)]
     behind = lax.ppermute(sent, "lon", [pair[::-1] for pair in west])

time: 48.1 us -> 48 us (level)
  no operation moved by 1% of the time
where the time goes in v4:
time: 48 us; the launch traced here: 47.7 us
  starting transfers between devices  27.2 us (57%)
  Pallas kernels  12.8 us (27%)
  blocking collectives  7.28 us (15%)
    ppermute x1, starting transfers between devices, local(): ahead_other = lax.ppermute(other, 'lon', west)  13 us
    pallas_call x6, Pallas kernels, call(): pl.pallas_call(body, out_shape=outs[0] if single else outs, in_specs=[pl....  12.8 us
    all_gather x2, blocking collectives, gather(): lax.all_gather(jnp.stack([part, other]), 'lev', tiled=True, axis_index_gr...  7.28 us
    ppermute x2, starting transfers between devices, local(): lax.ppermute(part, 'lev', swap)  6.78 us
    ppermute x1, starting transfers between devices, local(): behind = lax.ppermute(sent, 'lon', [pair[::-1] for pair in west])  4.03 us
    ppermute x1, starting transfers between devices, local(): ahead_edge = lax.ppermute(edge, 'lon', west)  3.36 us
  transfers between devices with their start and end apart: 5, of which 0 were waited for; matrix products, arithmetic and copies ran while one was open for 0% of the time, Pallas kernels for 16%

profile of v4, /device:TPU:1, one launch (start us, length us, event | category | flops | bytes accessed | tf_op | source)
XLA Modules:
  0.0 47.7 jit_solution(9153438807054840499)
XLA Ops:
  0.0 0.0 copy-start.5
  0.0 1.2 %shard_map.100 = (bf16[17,16,384]{2,1,0:T(8,128)(2,1)S(1)}, bf16[16,16,384]{2,1,0:T(8,128)(2,1)S(1)}, bf16[16,16,384]{2,1,0:T(8,128)(2,1)S(1)}, s32[16,128]{1,0:T(8,128)S(1)}) custom-call(s32[2]{0:T(128)} %shifts_hbm.3, s32[8]{0:T(128)} %counts_hbm.1, bf16[4,2,4,16,384]{4,3,2,1,0:T(8,128)(2,1)} %bitcast.10), custom_call_target="tpu_custom_call" | custom-call | flops 10000000000 | bytes 393256 | tf_op jit(solution)/shard_map/pallas_call | solution.py:288
  1.2 4.0 %collective-permute-start = (bf16[17,16,384]{2,1,0:T(8,128)(2,1)S(1)}, bf16[17,16,384]{2,1,0:T(8,128)(2,1)S(1)}, u32[]{:S(2)}, u32[]{:S(2)}) collective-permute-start(bf16[17,16,384]{2,1,0:T(8,128)(2,1)S(1)} %get-tuple-element.21), channel_id=1, source_target_pairs={{508,0},{0,4},{4,8},{8,12},{12,16},{16,20},{20,24},{24,28},{28,32}... | collective-permute-start | bytes 626696 | tf_op jit(solution)/shard_map/ppermute | solution.py:342
  5.2 0.0 copy-start.4
  5.3 13.0 %collective-permute-start.2 = (bf16[16,16,384]{2,1,0:T(8,128)(2,1)S(1)}, bf16[16,16,384]{2,1,0:T(8,128)(2,1)S(1)}, u32[]{:S(2)}, u32[]{:S(2)}) collective-permute-start(bf16[16,16,384]{2,1,0:T(8,128)(2,1)S(1)} %get-tuple-element.19.other_ref.own_ref), channel_id=1, source_target_pairs={{0,508},{4,0},{8,4},{12,8},{16,12},{20,16},{24,20},{28,24},{32,28}... | collective-permute-start | bytes 589832 | tf_op jit(solution)/shard_map/ppermute | solution.py:343
  18.3 3.4 %collective-permute-start.1 = (bf16[16,16,384]{2,1,0:T(8,128)(2,1)S(1)}, bf16[16,16,384]{2,1,0:T(8,128)(2,1)S(1)}, u32[]{:S(2)}, u32[]{:S(2)}) collective-permute-start(bf16[16,16,384]{2,1,0:T(8,128)(2,1)S(1)} %get-tuple-element.18.edge_ref.own_ref), channel_id=1, source_target_pairs={{0,508},{4,0},{8,4},{12,8},{16,12},{20,16},{24,20},{28,24},{32,28}... | collective-permute-start | bytes 589832 | tf_op jit(solution)/shard_map/ppermute | solution.py:348
  21.7 0.0 copy-done.5
  21.7 0.0 copy-done.4
  21.7 0.0 copy-start.6
  21.7 1.2 %shard_map.101 = (bf16[3,256,384]{2,1,0:T(8,128)(2,1)S(1)}, bf16[3,256,384]{2,1,0:T(8,128)(2,1)S(1)}) custom-call(bf16[16,16,384]{2,1,0:T(8,128)(2,1)S(1)} %get-tuple-element.18.edge_ref.own_ref, bf16[16,16,384]{2,1,0:T(8,128)(2,1)S(1)} %get-tuple-element.19.other_ref.own_ref, f32[3,384]{1,0:T(4,128)S(1)} %copy-done.4, bf16[3,384,384]{2,1,0:T(8,128)(2,1)S(1)} %copy-done.5), custom_call_target="tpu_custom_call" | custom-call | flops 1000000000 | bytes 1282560 | tf_op jit(solution)/shard_map/pallas_call | solution.py:288
  22.9 0.0 collective-permute-done.2.ahead_ref
  22.9 0.0 collective-permute-done.behind_ref
  22.9 0.0 copy-done.6
  22.9 1.6 %shard_map.102 = (bf16[256,384]{1,0:T(8,128)(2,1)S(1)}, bf16[256,384]{1,0:T(8,128)(2,1)S(1)}) custom-call(s32[16,128]{1,0:T(8,128)S(1)} %get-tuple-element.17.facts_ref, s32[8,128]{1,0:T(8,128)S(1)} %broadcast_in_dim.3.anchor_ref, bf16[16,16,384]{2,1,0:T(8,128)(2,1)S(1)} %get-tuple-element.19.other_ref.own_ref, ...), custom_call_target="tpu_custom_call" | custom-call | flops 1000000000 | bytes 2388480 | tf_op jit(solution)/shard_map/pallas_call | solution.py:288
  24.6 4.5 %collective-permute-start.3 = (bf16[256,384]{1,0:T(8,128)(2,1)S(1)}, bf16[256,384]{1,0:T(8,128)(2,1)S(1)}, u32[]{:S(2)}, u32[]{:S(2)}) collective-permute-start(bf16[256,384]{1,0:T(8,128)(2,1)S(1)} %get-tuple-element.26.normed_ref), channel_id=1, source_target_pairs={{0,2},{1,3},{2,0},{3,1},{4,6},{5,7},{6,4},{7,5},{8,10},{9,11},{10,... | collective-permute-start | bytes 589832 | tf_op jit(solution)/shard_map/ppermute | solution.py:371
  29.1 0.0 collective-permute-done.1.ahead_ref
  29.1 0.0 copy-start.2
  29.1 1.6 %shard_map.103 = (bf16[256,384]{1,0:T(8,128)(2,1)S(1)}, bf16[256,384]{1,0:T(8,128)(2,1)S(1)}) custom-call(s32[16,128]{1,0:T(8,128)S(1)} %get-tuple-element.17.facts_ref, s32[8,128]{1,0:T(8,128)S(1)} %broadcast_in_dim.3.anchor_ref, bf16[16,16,384]{2,1,0:T(8,128)(2,1)S(1)} %get-tuple-element.18.edge_ref.own_ref, ...), custom_call_target="tpu_custom_call" | custom-call | flops 1000000000 | bytes 2585088 | tf_op jit(solution)/shard_map/pallas_call | solution.py:288
  30.8 2.2 %collective-permute-start.4 = (bf16[256,384]{1,0:T(8,128)(2,1)S(1)}, bf16[256,384]{1,0:T(8,128)(2,1)S(1)}, u32[]{:S(2)}, u32[]{:S(2)}) collective-permute-start(bf16[256,384]{1,0:T(8,128)(2,1)S(1)} %get-tuple-element.25.normed_ref), channel_id=1, source_target_pairs={{0,2},{1,3},{2,0},{3,1},{4,6},{5,7},{6,4},{7,5},{8,10},{9,11},{10,... | collective-permute-start | bytes 589832 | tf_op jit(solution)/shard_map/ppermute | solution.py:371
  33.0 0.0 collective-permute-done.3
  33.0 0.0 copy-start
  33.1 0.0 copy-start.1
  33.1 0.0 copy-start.3
  33.1 4.4 %all_gather.6.gathered_ref = bf16[4,256,384]{2,1,0:T(8,128)(2,1)S(1)} all-gather(bf16[2,256,384]{2,1,0:T(8,128)(2,1)S(1)} %pad_maximum_fusion), channel_id=1, replica_groups={{0,1},{2,3},{4,5},{6,7},{8,9},{10,11},{12,13},{14,15},{16,17},{18,19},{..., dimensions={0}, use_global_device_ids=true | all-gather | bytes 1179648 | tf_op jit(solution)/shard_map/all_gather | solution.py:369
  37.5 0.0 copy-done.2
  37.5 0.0 copy-done
  37.5 0.0 copy-done.1
  37.5 0.0 copy-done.3
  37.5 3.2 %shard_map.104.first_ref = bf16[4,64,384]{2,1,0:T(8,128)(2,1)S(1)} custom-call(s32[16,128]{1,0:T(8,128)S(1)} %get-tuple-element.17.facts_ref, s32[8,128]{1,0:T(8,128)S(1)} %broadcast_in_dim.3.anchor_ref, bf16[256,384]{1,0:T(8,128)(2,1)S(1)} %get-tuple-element.23._.resident_ref, bf16[256,384]{1,0:T(8,128)(2,1)S(1)} %get-tuple-element.26.normed_ref, ...), custom_call_target="tpu_custom_call" | custom-call | flops 1000000000 | bytes 3555840 | tf_op jit(solution)/shard_map/pallas_call | solution.py:288
  40.7 0.0 collective-permute-done.4
  40.8 2.9 %all_gather.7.gathered_ref = bf16[4,256,384]{2,1,0:T(8,128)(2,1)S(1)} all-gather(bf16[2,256,384]{2,1,0:T(8,128)(2,1)S(1)} %pad_maximum_fusion.1), channel_id=1, replica_groups={{0,1},{2,3},{4,5},{6,7},{8,9},{10,11},{12,13},{14,15},{16,17},{18,19},{..., dimensions={0}, use_global_device_ids=true | all-gather | bytes 1179648 | tf_op jit(solution)/shard_map/all_gather | solution.py:369
  43.7 4.0 %shard_map.105 = bf16[4,2,64,384]{3,2,1,0:T(8,128)(2,1)} custom-call(s32[2]{0:T(128)} %shifts_hbm.3, s32[16,128]{1,0:T(8,128)S(1)} %get-tuple-element.17.facts_ref, s32[8,128]{1,0:T(8,128)S(1)} %broadcast_in_dim.3.anchor_ref, bf16[256,384]{1,0:T(8,128)(2,1)S(1)} %get-tuple-element.24.resident_ref, bf16[256,384]{1,0:T(8,128)(2,1)S(1)} %get-tuple-element.25.normed_ref, ...), custom_call_target="tpu_custom_call" | custom-call | flops 1000000000 | bytes 3752456 | tf_op jit(solution)/shard_map/pallas_call | solution.py:288
  (3 shorter events, 0.1 us)
Async XLA Ops:
  0.0 21.7 %copy-start.5 = (bf16[3,384,384]{2,1,0:T(8,128)(2,1)S(1)}, bf16[3,384,384]{2,1,0:T(8,128)(2,1)}, u32[]{:S(2)}) copy-start(bf16[3,384,384]{2,1,0:T(8,128)(2,1)} %qkv_ref.7) | copy-start | bytes 2654212
  1.2 21.7 %collective-permute-start = (bf16[17,16,384]{2,1,0:T(8,128)(2,1)S(1)}, bf16[17,16,384]{2,1,0:T(8,128)(2,1)S(1)}, u32[]{:S(2)}, u32[]{:S(2)}) collective-permute-start(bf16[17,16,384]{2,1,0:T(8,128)(2,1)S(1)} %get-tuple-element.21), channel_id=1, source_target_pairs={{508,0},{0,4},{4,8},{8,12},{12,16},{16,20},{20,24},{24,28},{28,32}... | collective-permute-start | bytes 626696 | tf_op jit(solution)/shard_map/ppermute | solution.py:342
  5.2 16.5 %copy-start.4 = (f32[3,384]{1,0:T(4,128)S(1)}, f32[3,384]{1,0:T(4,128)}, u32[]{:S(2)}) copy-start(f32[3,384]{1,0:T(4,128)} %gains_ref.9) | copy-start | bytes 13828
  5.3 17.6 %collective-permute-start.2 = (bf16[16,16,384]{2,1,0:T(8,128)(2,1)S(1)}, bf16[16,16,384]{2,1,0:T(8,128)(2,1)S(1)}, u32[]{:S(2)}, u32[]{:S(2)}) collective-permute-start(bf16[16,16,384]{2,1,0:T(8,128)(2,1)S(1)} %get-tuple-element.19.other_ref.own_ref), channel_id=1, source_target_pairs={{0,508},{4,0},{8,4},{12,8},{16,12},{20,16},{24,20},{28,24},{32,28}... | collective-permute-start | bytes 589832 | tf_op jit(solution)/shard_map/ppermute | solution.py:343
  18.3 10.8 %collective-permute-start.1 = (bf16[16,16,384]{2,1,0:T(8,128)(2,1)S(1)}, bf16[16,16,384]{2,1,0:T(8,128)(2,1)S(1)}, u32[]{:S(2)}, u32[]{:S(2)}) collective-permute-start(bf16[16,16,384]{2,1,0:T(8,128)(2,1)S(1)} %get-tuple-element.18.edge_ref.own_ref), channel_id=1, source_target_pairs={{0,508},{4,0},{8,4},{12,8},{16,12},{20,16},{24,20},{28,24},{32,28}... | collective-permute-start | bytes 589832 | tf_op jit(solution)/shard_map/ppermute | solution.py:348
  21.7 1.2 %copy-start.6 = (bf16[384,384]{1,0:T(8,128)(2,1)S(1)}, bf16[384,384]{1,0:T(8,128)(2,1)}, u32[]{:S(2)}) copy-start(bf16[384,384]{1,0:T(8,128)(2,1)} %out_w_ref.5) | copy-start | bytes 884740
  24.6 8.4 %collective-permute-start.3 = (bf16[256,384]{1,0:T(8,128)(2,1)S(1)}, bf16[256,384]{1,0:T(8,128)(2,1)S(1)}, u32[]{:S(2)}, u32[]{:S(2)}) collective-permute-start(bf16[256,384]{1,0:T(8,128)(2,1)S(1)} %get-tuple-element.26.normed_ref), channel_id=1, source_target_pairs={{0,2},{1,3},{2,0},{3,1},{4,6},{5,7},{6,4},{7,5},{8,10},{9,11},{10,... | collective-permute-start | bytes 589832 | tf_op jit(solution)/shard_map/ppermute | solution.py:371
  29.1 8.4 %copy-start.2 = (bf16[768,384]{1,0:T(8,128)(2,1)S(1)}, bf16[768,384]{1,0:T(8,128)(2,1)}, u32[]{:S(2)}) copy-start(bf16[768,384]{1,0:T(8,128)(2,1)} %mlp_ref.3) | copy-start | bytes 1769476
  30.8 9.9 %collective-permute-start.4 = (bf16[256,384]{1,0:T(8,128)(2,1)S(1)}, bf16[256,384]{1,0:T(8,128)(2,1)S(1)}, u32[]{:S(2)}, u32[]{:S(2)}) collective-permute-start(bf16[256,384]{1,0:T(8,128)(2,1)S(1)} %get-tuple-element.25.normed_ref), channel_id=1, source_target_pairs={{0,2},{1,3},{2,0},{3,1},{4,6},{5,7},{6,4},{7,5},{8,10},{9,11},{10,... | collective-permute-start | bytes 589832 | tf_op jit(solution)/shard_map/ppermute | solution.py:371
  33.0 4.5 %copy-start = (bf16[3,384,384]{2,1,0:T(8,128)(2,1)S(1)}, bf16[3,384,384]{2,1,0:T(8,128)(2,1)}, u32[]{:S(2)}) copy-start(bf16[3,384,384]{2,1,0:T(8,128)(2,1)} %qkv_ref.9) | copy-start | bytes 2654212
  33.1 4.4 %copy-start.1 = (bf16[384,768]{1,0:T(8,128)(2,1)S(1)}, bf16[384,768]{1,0:T(8,128)(2,1)}, u32[]{:S(2)}) copy-start(bf16[384,768]{1,0:T(8,128)(2,1)} %in_ref.3) | copy-start | bytes 1769476
  33.1 4.4 %copy-start.3 = (bf16[384,384]{1,0:T(8,128)(2,1)S(1)}, bf16[384,384]{1,0:T(8,128)(2,1)}, u32[]{:S(2)}) copy-start(bf16[384,384]{1,0:T(8,128)(2,1)} %out_w_ref.7) | copy-start | bytes 884740

commit v5 on v4

--- a/solution.py
+++ b/solution.py
@@ -29,10 +29,14 @@
     return jnp.dot(left, right, preferred_element_type=F32)
 
 
-def attend(units, allowed, head_size):
+def project_queries(normed, weights):
+    scale = math.log2(math.e) / math.sqrt(weights.shape[1] // HEADS)
+    return (dot32(normed, weights) * scale).astype(BF16)
+
+
+def attend(units, allowed, head_size, exp_type):
     count, width = units[0][0].shape
     per = LANES // head_size
-    scale = math.log2(math.e) / math.sqrt(head_size)
     head_of_lane = lax.broadcasted_iota(jnp.int32, (count, LANES), 1) // head_size
     both = jnp.concatenate([head_of_lane, head_of_lane], axis=1)
     ones = jnp.ones((units[0][1].shape[0], LANES), BF16)
@@ -51,7 +55,7 @@
     for score in scores:
         score = jnp.where(allowed[None], score.reshape(per, count, -1), -jnp.inf)
         highest = jnp.max(score, axis=-1, keepdims=True)
-        weights.append(jnp.exp2((score - highest) * scale).astype(BF16).reshape(per * count, -1))
+        weights.append(jnp.exp2((score - highest).astype(exp_type)).astype(BF16).reshape(per * count, -1))
     mixes = [
         dot32(weight, jnp.concatenate([values, ones], axis=1)).reshape(per, count, 2 * LANES)
         for weight, (_, _, values) in zip(weights, jobs)
@@ -121,7 +125,8 @@
     ]
     for n in range(3):
         for part, out_ref in zip(normed, outs):
-            out_ref[n] = dot32(part, qkv_ref[n]).astype(BF16)
+            project = dot32 if n > 0 else project_queries
+            out_ref[n] = project(part, qkv_ref[n]).astype(BF16)
 
 
 def window_block(
@@ -154,7 +159,7 @@
                 jnp.concatenate([done_ref[2, at], values[at]], axis=0),
             )
         )
-    mixed = attend(units, allowed, width // HEADS)
+    mixed = attend(units, allowed, width // HEADS, F32)
     resident = (own + dot32(jnp.concatenate(mixed, axis=0), out_w_ref[...])).astype(BF16)
     result_ref[...] = resident
     normed_ref[...] = layer_norm(resident.astype(F32), gains_ref[1:2])
@@ -193,13 +198,9 @@
     )
 
 
-def column_attend(normed_ref, gathered_ref, qkv_ref):
-    parts, tokens, width = gathered_ref.shape
-    total = parts * tokens
-    normed = gathered_ref[...].reshape(total, width)
-    queries = dot32(normed_ref[...], qkv_ref[0]).astype(BF16)
-    keys, values = [dot32(normed, qkv_ref[n]).astype(BF16) for n in (1, 2)]
-
+def column_attend(queries, keys, values):
+    tokens, width = queries.shape
+    total = keys.shape[0]
     span = WIN_ROWS * WIN_LON
     levels = tokens // span
     all_levels = total // span
@@ -221,7 +222,7 @@
             )
             for row in (first, first + 1)
         ]
-        mixed += attend(units, allowed, width // HEADS)
+        mixed += attend(units, allowed, width // HEADS, BF16)
     mixed = jnp.concatenate([part.reshape(levels, 1, WIN_LON, width) for part in mixed], axis=1)
     return mixed.reshape(tokens, width)
 
@@ -252,18 +253,35 @@
     facts_ref, anchor_ref, resident_ref, normed_ref, gathered_ref, gains_ref, qkv_ref, out_w_ref, in_ref, mlp_ref,
     result_ref,
 ):
-    mixed = column_attend(normed_ref, gathered_ref, qkv_ref)
+    queries = project_queries(normed_ref[...], qkv_ref[0])
+    gathered = gathered_ref[...].reshape(-1, resident_ref.shape[1])
+    keys, values = [dot32(gathered, qkv_ref[n]).astype(BF16) for n in (1, 2)]
+    mixed = column_attend(queries, keys, values)
     result = feed_forward(mixed, resident_ref, gains_ref, out_w_ref, in_ref, mlp_ref)
     result_ref[...] = live_cells(facts_ref, anchor_ref, BOTH_COUNTS, result)
 
 
+def column_own_kernel(normed_ref, qkv_ref, _, result_ref):
+    normed = normed_ref[...]
+    result_ref[0] = project_queries(normed, qkv_ref[0])
+    for n in (1, 2):
+        result_ref[n] = dot32(normed, qkv_ref[n]).astype(BF16)
+
+
 def column_last_kernel(
-    shifts_hbm, facts_ref, anchor_ref, resident_ref, normed_ref, gathered_ref, first_ref, gains_ref, qkv_ref,
-    out_w_ref, in_ref, mlp_ref, result_ref, stage_ref, shifts_ref, sems,
+    core_ref, shifts_hbm, facts_ref, anchor_ref, resident_ref, done_ref, swapped_ref, gathered_ref, first_ref,
+    gains_ref, qkv_ref, out_w_ref, in_ref, mlp_ref, result_ref, stage_ref, shifts_ref, sems,
 ):
     shifts_copy = pltpu.make_async_copy(shifts_hbm, shifts_ref, sems.at[2])
     shifts_copy.start()
-    mixed = column_attend(normed_ref, gathered_ref, qkv_ref)
+    parts, tokens, width = gathered_ref.shape
+    half = parts // CORES
+    partner = gathered_ref[pl.ds((1 - core_ref[0]) * half, half)].reshape(half * tokens, width)
+    rest = jnp.concatenate([swapped_ref[...], partner], axis=0)
+    keys, values = [
+        jnp.concatenate([done_ref[n], dot32(rest, qkv_ref[n]).astype(BF16)], axis=0) for n in (1, 2)
+    ]
+    mixed = column_attend(done_ref[0], keys, values)
     shifts_copy.wait()
     block = edge_block(shifts_ref)
     first = pltpu.make_async_copy(first_ref, result_ref.at[:, 1 - block], sems.at[0])
@@ -377,19 +395,28 @@
         [facts, anchor, resident_other, normed_other, gather(normed_other, swapped_other)] + weights,
         10**9,
     )
+    done = call(
+        column_own_kernel,
+        [three],
+        [],
+        [normed_edge, column_qkv, first],
+        10**9,
+        spaces=[pltpu.VMEM, pltpu.VMEM, pl.ANY],
+    )
     first, swapped_edge = lax.optimization_barrier((first, swapped_edge))
+    core = (lax.axis_index("lev") % CORES).astype(jnp.int32).reshape(1)
     result = call(
         column_last_kernel,
         [jax.ShapeDtypeStruct((levels, blocks, tokens, width), BF16)],
-        [],
-        [shifts, facts, anchor, resident_edge, normed_edge, gather(normed_edge, swapped_edge), first] + weights,
+        [core],
+        [shifts, facts, anchor, resident_edge, done, swapped_edge, gather(normed_edge, swapped_edge), first] + weights,
         10**9,
         [
             pltpu.VMEM((levels, tokens, width), BF16),
             pltpu.SMEM(shifts.shape, jnp.int32),
             pltpu.SemaphoreType.DMA((3,)),
         ],
-        [pltpu.HBM] + [pltpu.VMEM] * (6 + len(weights)),
+        [pltpu.HBM] + [pltpu.VMEM] * (7 + len(weights)),
         out_spaces=[pltpu.HBM],
     )
     return result.reshape(fields.shape)

time: 48 us -> 47.9 us (level)
    pallas_call x6 -> x7, Pallas kernels: 12.8 us -> 13.1 us  [call(): pl.pallas_call(body, out_shape=outs[0] if single else outs, in_specs=[pl....]
  transfers between devices with their start and end apart: 5 -> 5, of which waited for: 0 -> 0; matrix products, arithmetic and copies ran while one was open for 0% -> 0% of each run, Pallas kernels for 16% -> 17%
where the time goes in v5:
time: 47.9 us; the launch traced here: 47.6 us
  starting transfers between devices  27.2 us (57%)
  Pallas kernels  13.1 us (27%)
  blocking collectives  6.87 us (14%)
    pallas_call x7, Pallas kernels, call(): pl.pallas_call(body, out_shape=outs[0] if single else outs, in_specs=[pl....  13.1 us
    ppermute x1, starting transfers between devices, local(): ahead_other = lax.ppermute(other, 'lon', west)  13 us
    all_gather x2, blocking collectives, gather(): lax.all_gather(jnp.stack([part, other]), 'lev', tiled=True, axis_index_gr...  6.87 us
    ppermute x2, starting transfers between devices, local(): lax.ppermute(part, 'lev', swap)  6.79 us
    ppermute x1, starting transfers between devices, local(): behind = lax.ppermute(sent, 'lon', [pair[::-1] for pair in west])  4.03 us
    ppermute x1, starting transfers between devices, local(): ahead_edge = lax.ppermute(edge, 'lon', west)  3.36 us
  transfers between devices with their start and end apart: 5, of which 0 were waited for; matrix products, arithmetic and copies ran while one was open for 0% of the time, Pallas kernels for 17%

profile of v5, /device:TPU:1, one launch (start us, length us, event | category | flops | bytes accessed | tf_op | source)
XLA Modules:
  0.0 47.6 jit_solution(16714689167945302992)
XLA Ops:
  0.0 0.0 copy-start.5
  0.0 1.2 %shard_map.100 = (bf16[17,16,384]{2,1,0:T(8,128)(2,1)S(1)}, bf16[16,16,384]{2,1,0:T(8,128)(2,1)S(1)}, bf16[16,16,384]{2,1,0:T(8,128)(2,1)S(1)}, s32[16,128]{1,0:T(8,128)S(1)}) custom-call(s32[2]{0:T(128)} %shifts_hbm.3, s32[8]{0:T(128)} %counts_hbm.1, bf16[4,2,4,16,384]{4,3,2,1,0:T(8,128)(2,1)} %bitcast.11), custom_call_target="tpu_custom_call" | custom-call | flops 10000000000 | bytes 393256 | tf_op jit(solution)/shard_map/pallas_call | solution.py:306
  1.2 4.0 %collective-permute-start = (bf16[17,16,384]{2,1,0:T(8,128)(2,1)S(1)}, bf16[17,16,384]{2,1,0:T(8,128)(2,1)S(1)}, u32[]{:S(2)}, u32[]{:S(2)}) collective-permute-start(bf16[17,16,384]{2,1,0:T(8,128)(2,1)S(1)} %get-tuple-element.21), channel_id=1, source_target_pairs={{508,0},{0,4},{4,8},{8,12},{12,16},{16,20},{20,24},{24,28},{28,32}... | collective-permute-start | bytes 626696 | tf_op jit(solution)/shard_map/ppermute | solution.py:360
  5.2 0.0 copy-start.4
  5.3 13.0 %collective-permute-start.2 = (bf16[16,16,384]{2,1,0:T(8,128)(2,1)S(1)}, bf16[16,16,384]{2,1,0:T(8,128)(2,1)S(1)}, u32[]{:S(2)}, u32[]{:S(2)}) collective-permute-start(bf16[16,16,384]{2,1,0:T(8,128)(2,1)S(1)} %get-tuple-element.19.other_ref.own_ref), channel_id=1, source_target_pairs={{0,508},{4,0},{8,4},{12,8},{16,12},{20,16},{24,20},{28,24},{32,28}... | collective-permute-start | bytes 589832 | tf_op jit(solution)/shard_map/ppermute | solution.py:361
  18.3 3.4 %collective-permute-start.1 = (bf16[16,16,384]{2,1,0:T(8,128)(2,1)S(1)}, bf16[16,16,384]{2,1,0:T(8,128)(2,1)S(1)}, u32[]{:S(2)}, u32[]{:S(2)}) collective-permute-start(bf16[16,16,384]{2,1,0:T(8,128)(2,1)S(1)} %get-tuple-element.18.edge_ref.own_ref), channel_id=1, source_target_pairs={{0,508},{4,0},{8,4},{12,8},{16,12},{20,16},{24,20},{28,24},{32,28}... | collective-permute-start | bytes 589832 | tf_op jit(solution)/shard_map/ppermute | solution.py:366
  21.7 0.0 copy-done.5
  21.7 0.0 copy-done.4
  21.7 0.0 copy-start.6
  21.7 1.2 %shard_map.101 = (bf16[3,256,384]{2,1,0:T(8,128)(2,1)S(1)}, bf16[3,256,384]{2,1,0:T(8,128)(2,1)S(1)}) custom-call(bf16[16,16,384]{2,1,0:T(8,128)(2,1)S(1)} %get-tuple-element.18.edge_ref.own_ref, bf16[16,16,384]{2,1,0:T(8,128)(2,1)S(1)} %get-tuple-element.19.other_ref.own_ref, f32[3,384]{1,0:T(4,128)S(1)} %copy-done.4, bf16[3,384,384]{2,1,0:T(8,128)(2,1)S(1)} %copy-done.5), custom_call_target="tpu_custom_call" | custom-call | flops 1000000000 | bytes 1282560 | tf_op jit(solution)/shard_map/pallas_call | solution.py:306
  22.9 0.0 collective-permute-done.2.ahead_ref
  22.9 0.0 collective-permute-done.behind_ref
  22.9 0.0 copy-done.6
  22.9 1.6 %shard_map.102 = (bf16[256,384]{1,0:T(8,128)(2,1)S(1)}, bf16[256,384]{1,0:T(8,128)(2,1)S(1)}) custom-call(s32[16,128]{1,0:T(8,128)S(1)} %get-tuple-element.17.facts_ref, s32[8,128]{1,0:T(8,128)S(1)} %broadcast_in_dim.3.anchor_ref, bf16[16,16,384]{2,1,0:T(8,128)(2,1)S(1)} %get-tuple-element.19.other_ref.own_ref, ...), custom_call_target="tpu_custom_call" | custom-call | flops 1000000000 | bytes 2388480 | tf_op jit(solution)/shard_map/pallas_call | solution.py:306
  24.6 4.5 %collective-permute-start.3 = (bf16[256,384]{1,0:T(8,128)(2,1)S(1)}, bf16[256,384]{1,0:T(8,128)(2,1)S(1)}, u32[]{:S(2)}, u32[]{:S(2)}) collective-permute-start(bf16[256,384]{1,0:T(8,128)(2,1)S(1)} %get-tuple-element.26.normed_ref), channel_id=1, source_target_pairs={{0,2},{1,3},{2,0},{3,1},{4,6},{5,7},{6,4},{7,5},{8,10},{9,11},{10,... | collective-permute-start | bytes 589832 | tf_op jit(solution)/shard_map/ppermute | solution.py:389
  29.1 0.0 collective-permute-done.1.ahead_ref
  29.1 0.0 copy-start.2
  29.2 1.6 %shard_map.103 = (bf16[256,384]{1,0:T(8,128)(2,1)S(1)}, bf16[256,384]{1,0:T(8,128)(2,1)S(1)}) custom-call(s32[16,128]{1,0:T(8,128)S(1)} %get-tuple-element.17.facts_ref, s32[8,128]{1,0:T(8,128)S(1)} %broadcast_in_dim.3.anchor_ref, bf16[16,16,384]{2,1,0:T(8,128)(2,1)S(1)} %get-tuple-element.18.edge_ref.own_ref, ...), custom_call_target="tpu_custom_call" | custom-call | flops 1000000000 | bytes 2585088 | tf_op jit(solution)/shard_map/pallas_call | solution.py:306
  30.8 2.3 %collective-permute-start.4 = (bf16[256,384]{1,0:T(8,128)(2,1)S(1)}, bf16[256,384]{1,0:T(8,128)(2,1)S(1)}, u32[]{:S(2)}, u32[]{:S(2)}) collective-permute-start(bf16[256,384]{1,0:T(8,128)(2,1)S(1)} %get-tuple-element.25.normed_ref), channel_id=1, source_target_pairs={{0,2},{1,3},{2,0},{3,1},{4,6},{5,7},{6,4},{7,5},{8,10},{9,11},{10,... | collective-permute-start | bytes 589832 | tf_op jit(solution)/shard_map/ppermute | solution.py:389
  33.1 0.0 collective-permute-done.3
  33.1 0.0 copy-start
  33.1 0.0 copy-start.1
  33.1 0.0 copy-start.3
  33.2 4.4 %all_gather.6.gathered_ref = bf16[4,256,384]{2,1,0:T(8,128)(2,1)S(1)} all-gather(bf16[2,256,384]{2,1,0:T(8,128)(2,1)S(1)} %pad_maximum_fusion), channel_id=1, replica_groups={{0,1},{2,3},{4,5},{6,7},{8,9},{10,11},{12,13},{14,15},{16,17},{18,19},{..., dimensions={0}, use_global_device_ids=true | all-gather | bytes 1179648 | tf_op jit(solution)/shard_map/all_gather | solution.py:387
  37.5 0.0 copy-done.2
  37.5 0.0 copy-done
  37.5 0.0 copy-done.1
  37.5 0.0 copy-done.3
  37.5 3.1 %shard_map.104._.first_ref = bf16[4,64,384]{2,1,0:T(8,128)(2,1)S(1)} custom-call(s32[16,128]{1,0:T(8,128)S(1)} %get-tuple-element.17.facts_ref, s32[8,128]{1,0:T(8,128)S(1)} %broadcast_in_dim.3.anchor_ref, bf16[256,384]{1,0:T(8,128)(2,1)S(1)} %get-tuple-element.23._.resident_ref, bf16[256,384]{1,0:T(8,128)(2,1)S(1)} %get-tuple-element.26.normed_ref, ...), custom_call_target="tpu_custom_call" | custom-call | flops 1000000000 | bytes 3555840 | tf_op jit(solution)/shard_map/pallas_call | solution.py:306
  40.6 0.5 %shard_map.105.done_ref = bf16[3,256,384]{2,1,0:T(8,128)(2,1)S(1)} custom-call(bf16[256,384]{1,0:T(8,128)(2,1)S(1)} %get-tuple-element.25.normed_ref, bf16[3,384,384]{2,1,0:T(8,128)(2,1)S(1)} %copy-done, bf16[4,64,384]{2,1,0:T(8,128)(2,1)S(1)} %shard_map.104._.first_ref), custom_call_target="tpu_custom_call" | custom-call | flops 1000000000 | bytes 1277952 | tf_op jit(solution)/shard_map/pallas_call | solution.py:306
  41.1 0.0 collective-permute-done.4.swapped_ref
  41.2 2.5 %all_gather.7.gathered_ref = bf16[4,256,384]{2,1,0:T(8,128)(2,1)S(1)} all-gather(bf16[2,256,384]{2,1,0:T(8,128)(2,1)S(1)} %pad_maximum_fusion.1), channel_id=1, replica_groups={{0,1},{2,3},{4,5},{6,7},{8,9},{10,11},{12,13},{14,15},{16,17},{18,19},{..., dimensions={0}, use_global_device_ids=true | all-gather | bytes 1179648 | tf_op jit(solution)/shard_map/all_gather | solution.py:387
  43.7 3.9 %shard_map.106 = bf16[4,2,64,384]{3,2,1,0:T(8,128)(2,1)} custom-call(s32[1]{0:T(128)} %bitcast.core_ref, s32[2]{0:T(128)} %shifts_hbm.3, s32[16,128]{1,0:T(8,128)S(1)} %get-tuple-element.17.facts_ref, s32[8,128]{1,0:T(8,128)S(1)} %broadcast_in_dim.3.anchor_ref, bf16[256,384]{1,0:T(8,128)(2,1)S(1)} %get-tuple-element.24.resident_ref, ...), custom_call_target="tpu_custom_call" | custom-call | flops 1000000000 | bytes 4342280 | tf_op jit(solution)/shard_map/pallas_call | solution.py:306
  (3 shorter events, 0.1 us)
Async XLA Ops:
  0.0 21.7 %copy-start.5 = (bf16[3,384,384]{2,1,0:T(8,128)(2,1)S(1)}, bf16[3,384,384]{2,1,0:T(8,128)(2,1)}, u32[]{:S(2)}) copy-start(bf16[3,384,384]{2,1,0:T(8,128)(2,1)} %qkv_ref.8) | copy-start | bytes 2654212
  1.2 21.7 %collective-permute-start = (bf16[17,16,384]{2,1,0:T(8,128)(2,1)S(1)}, bf16[17,16,384]{2,1,0:T(8,128)(2,1)S(1)}, u32[]{:S(2)}, u32[]{:S(2)}) collective-permute-start(bf16[17,16,384]{2,1,0:T(8,128)(2,1)S(1)} %get-tuple-element.21), channel_id=1, source_target_pairs={{508,0},{0,4},{4,8},{8,12},{12,16},{16,20},{20,24},{24,28},{28,32}... | collective-permute-start | bytes 626696 | tf_op jit(solution)/shard_map/ppermute | solution.py:360
  5.2 16.5 %copy-start.4 = (f32[3,384]{1,0:T(4,128)S(1)}, f32[3,384]{1,0:T(4,128)}, u32[]{:S(2)}) copy-start(f32[3,384]{1,0:T(4,128)} %gains_ref.9) | copy-start | bytes 13828
  5.3 17.6 %collective-permute-start.2 = (bf16[16,16,384]{2,1,0:T(8,128)(2,1)S(1)}, bf16[16,16,384]{2,1,0:T(8,128)(2,1)S(1)}, u32[]{:S(2)}, u32[]{:S(2)}) collective-permute-start(bf16[16,16,384]{2,1,0:T(8,128)(2,1)S(1)} %get-tuple-element.19.other_ref.own_ref), channel_id=1, source_target_pairs={{0,508},{4,0},{8,4},{12,8},{16,12},{20,16},{24,20},{28,24},{32,28}... | collective-permute-start | bytes 589832 | tf_op jit(solution)/shard_map/ppermute | solution.py:361
  18.3 10.8 %collective-permute-start.1 = (bf16[16,16,384]{2,1,0:T(8,128)(2,1)S(1)}, bf16[16,16,384]{2,1,0:T(8,128)(2,1)S(1)}, u32[]{:S(2)}, u32[]{:S(2)}) collective-permute-start(bf16[16,16,384]{2,1,0:T(8,128)(2,1)S(1)} %get-tuple-element.18.edge_ref.own_ref), channel_id=1, source_target_pairs={{0,508},{4,0},{8,4},{12,8},{16,12},{20,16},{24,20},{28,24},{32,28}... | collective-permute-start | bytes 589832 | tf_op jit(solution)/shard_map/ppermute | solution.py:366
  21.7 1.2 %copy-start.6 = (bf16[384,384]{1,0:T(8,128)(2,1)S(1)}, bf16[384,384]{1,0:T(8,128)(2,1)}, u32[]{:S(2)}) copy-start(bf16[384,384]{1,0:T(8,128)(2,1)} %out_w_ref.5) | copy-start | bytes 884740
  24.6 8.5 %collective-permute-start.3 = (bf16[256,384]{1,0:T(8,128)(2,1)S(1)}, bf16[256,384]{1,0:T(8,128)(2,1)S(1)}, u32[]{:S(2)}, u32[]{:S(2)}) collective-permute-start(bf16[256,384]{1,0:T(8,128)(2,1)S(1)} %get-tuple-element.26.normed_ref), channel_id=1, source_target_pairs={{0,2},{1,3},{2,0},{3,1},{4,6},{5,7},{6,4},{7,5},{8,10},{9,11},{10,... | collective-permute-start | bytes 589832 | tf_op jit(solution)/shard_map/ppermute | solution.py:389
  29.1 8.4 %copy-start.2 = (bf16[768,384]{1,0:T(8,128)(2,1)S(1)}, bf16[768,384]{1,0:T(8,128)(2,1)}, u32[]{:S(2)}) copy-start(bf16[768,384]{1,0:T(8,128)(2,1)} %mlp_ref.3) | copy-start | bytes 1769476
  30.8 10.3 %collective-permute-start.4 = (bf16[256,384]{1,0:T(8,128)(2,1)S(1)}, bf16[256,384]{1,0:T(8,128)(2,1)S(1)}, u32[]{:S(2)}, u32[]{:S(2)}) collective-permute-start(bf16[256,384]{1,0:T(8,128)(2,1)S(1)} %get-tuple-element.25.normed_ref), channel_id=1, source_target_pairs={{0,2},{1,3},{2,0},{3,1},{4,6},{5,7},{6,4},{7,5},{8,10},{9,11},{10,... | collective-permute-start | bytes 589832 | tf_op jit(solution)/shard_map/ppermute | solution.py:389
  33.1 4.5 %copy-start = (bf16[3,384,384]{2,1,0:T(8,128)(2,1)S(1)}, bf16[3,384,384]{2,1,0:T(8,128)(2,1)}, u32[]{:S(2)}) copy-start(bf16[3,384,384]{2,1,0:T(8,128)(2,1)} %qkv_ref.11) | copy-start | bytes 2654212
  33.1 4.4 %copy-start.1 = (bf16[384,768]{1,0:T(8,128)(2,1)S(1)}, bf16[384,768]{1,0:T(8,128)(2,1)}, u32[]{:S(2)}) copy-start(bf16[384,768]{1,0:T(8,128)(2,1)} %in_ref.3) | copy-start | bytes 1769476
  33.1 4.4 %copy-start.3 = (bf16[384,384]{1,0:T(8,128)(2,1)S(1)}, bf16[384,384]{1,0:T(8,128)(2,1)}, u32[]{:S(2)}) copy-start(bf16[384,384]{1,0:T(8,128)(2,1)} %out_w_ref.7) | copy-start | bytes 884740

commit v6 on v5

--- a/solution.py
+++ b/solution.py
@@ -159,10 +159,13 @@
                 jnp.concatenate([done_ref[2, at], values[at]], axis=0),
             )
         )
-    mixed = attend(units, allowed, width // HEADS, F32)
-    resident = (own + dot32(jnp.concatenate(mixed, axis=0), out_w_ref[...])).astype(BF16)
-    result_ref[...] = resident
-    normed_ref[...] = layer_norm(resident.astype(F32), gains_ref[1:2])
+    mixed = jnp.concatenate(attend(units, allowed, width // HEADS, F32), axis=0)
+    half = total // 2
+    halves = [slice(0, half), slice(half, total)]
+    resident = [(own[at] + dot32(mixed[at], out_w_ref[...])).astype(BF16) for at in halves]
+    for at, part in zip(halves, resident):
+        result_ref[at] = part
+        normed_ref[at] = layer_norm(part.astype(F32), gains_ref[1:2])
 
 
 def window_edge_kernel(

time: 47.9 us -> 47.8 us (level)
  no operation moved by 1% of the time
where the time goes in v6:
time: 47.8 us; the launch traced here: 47.5 us
  starting transfers between devices  27.2 us (57%)
  Pallas kernels  13 us (27%)
  blocking collectives  6.86 us (14%)
    ppermute x1, starting transfers between devices, local(): ahead_other = lax.ppermute(other, 'lon', west)  13 us
    pallas_call x7, Pallas kernels, call(): pl.pallas_call(body, out_shape=outs[0] if single else outs, in_specs=[pl....  13 us
    all_gather x2, blocking collectives, gather(): lax.all_gather(jnp.stack([part, other]), 'lev', tiled=True, axis_index_gr...  6.86 us
    ppermute x2, starting transfers between devices, local(): lax.ppermute(part, 'lev', swap)  6.79 us
    ppermute x1, starting transfers between devices, local(): behind = lax.ppermute(sent, 'lon', [pair[::-1] for pair in west])  4.03 us
    ppermute x1, starting transfers between devices, local(): ahead_edge = lax.ppermute(edge, 'lon', west)  3.36 us
  transfers between devices with their start and end apart: 5, of which 0 were waited for; matrix products, arithmetic and copies ran while one was open for 0% of the time, Pallas kernels for 17%

profile of v6, /device:TPU:1, one launch (start us, length us, event | category | flops | bytes accessed | tf_op | source)
XLA Modules:
  0.0 47.5 jit_solution(12733893173354378364)
XLA Ops:
  0.0 0.0 copy-start.5
  0.0 1.2 %shard_map.100 = (bf16[17,16,384]{2,1,0:T(8,128)(2,1)S(1)}, bf16[16,16,384]{2,1,0:T(8,128)(2,1)S(1)}, bf16[16,16,384]{2,1,0:T(8,128)(2,1)S(1)}, s32[16,128]{1,0:T(8,128)S(1)}) custom-call(s32[2]{0:T(128)} %shifts_hbm.3, s32[8]{0:T(128)} %counts_hbm.1, bf16[4,2,4,16,384]{4,3,2,1,0:T(8,128)(2,1)} %bitcast.11), custom_call_target="tpu_custom_call" | custom-call | flops 10000000000 | bytes 393256 | tf_op jit(solution)/shard_map/pallas_call | solution.py:309
  1.2 4.0 %collective-permute-start = (bf16[17,16,384]{2,1,0:T(8,128)(2,1)S(1)}, bf16[17,16,384]{2,1,0:T(8,128)(2,1)S(1)}, u32[]{:S(2)}, u32[]{:S(2)}) collective-permute-start(bf16[17,16,384]{2,1,0:T(8,128)(2,1)S(1)} %get-tuple-element.21), channel_id=1, source_target_pairs={{508,0},{0,4},{4,8},{8,12},{12,16},{16,20},{20,24},{24,28},{28,32}... | collective-permute-start | bytes 626696 | tf_op jit(solution)/shard_map/ppermute | solution.py:363
  5.2 0.0 copy-start.4
  5.3 13.0 %collective-permute-start.2 = (bf16[16,16,384]{2,1,0:T(8,128)(2,1)S(1)}, bf16[16,16,384]{2,1,0:T(8,128)(2,1)S(1)}, u32[]{:S(2)}, u32[]{:S(2)}) collective-permute-start(bf16[16,16,384]{2,1,0:T(8,128)(2,1)S(1)} %get-tuple-element.19.other_ref.own_ref), channel_id=1, source_target_pairs={{0,508},{4,0},{8,4},{12,8},{16,12},{20,16},{24,20},{28,24},{32,28}... | collective-permute-start | bytes 589832 | tf_op jit(solution)/shard_map/ppermute | solution.py:364
  18.3 3.4 %collective-permute-start.1 = (bf16[16,16,384]{2,1,0:T(8,128)(2,1)S(1)}, bf16[16,16,384]{2,1,0:T(8,128)(2,1)S(1)}, u32[]{:S(2)}, u32[]{:S(2)}) collective-permute-start(bf16[16,16,384]{2,1,0:T(8,128)(2,1)S(1)} %get-tuple-element.18.edge_ref.own_ref), channel_id=1, source_target_pairs={{0,508},{4,0},{8,4},{12,8},{16,12},{20,16},{24,20},{28,24},{32,28}... | collective-permute-start | bytes 589832 | tf_op jit(solution)/shard_map/ppermute | solution.py:369
  21.7 0.0 copy-done.5
  21.7 0.0 copy-done.4
  21.7 0.0 copy-start.6
  21.7 1.2 %shard_map.101 = (bf16[3,256,384]{2,1,0:T(8,128)(2,1)S(1)}, bf16[3,256,384]{2,1,0:T(8,128)(2,1)S(1)}) custom-call(bf16[16,16,384]{2,1,0:T(8,128)(2,1)S(1)} %get-tuple-element.18.edge_ref.own_ref, bf16[16,16,384]{2,1,0:T(8,128)(2,1)S(1)} %get-tuple-element.19.other_ref.own_ref, f32[3,384]{1,0:T(4,128)S(1)} %copy-done.4, bf16[3,384,384]{2,1,0:T(8,128)(2,1)S(1)} %copy-done.5), custom_call_target="tpu_custom_call" | custom-call | flops 1000000000 | bytes 1282560 | tf_op jit(solution)/shard_map/pallas_call | solution.py:309
  22.9 0.0 collective-permute-done.2.ahead_ref
  22.9 0.0 collective-permute-done.behind_ref
  22.9 0.0 copy-done.6
  22.9 1.6 %shard_map.102 = (bf16[256,384]{1,0:T(8,128)(2,1)S(1)}, bf16[256,384]{1,0:T(8,128)(2,1)S(1)}) custom-call(s32[16,128]{1,0:T(8,128)S(1)} %get-tuple-element.17.facts_ref, s32[8,128]{1,0:T(8,128)S(1)} %broadcast_in_dim.3.anchor_ref, bf16[16,16,384]{2,1,0:T(8,128)(2,1)S(1)} %get-tuple-element.19.other_ref.own_ref, ...), custom_call_target="tpu_custom_call" | custom-call | flops 1000000000 | bytes 2388480 | tf_op jit(solution)/shard_map/pallas_call | solution.py:309
  24.6 4.5 %collective-permute-start.3 = (bf16[256,384]{1,0:T(8,128)(2,1)S(1)}, bf16[256,384]{1,0:T(8,128)(2,1)S(1)}, u32[]{:S(2)}, u32[]{:S(2)}) collective-permute-start(bf16[256,384]{1,0:T(8,128)(2,1)S(1)} %get-tuple-element.26.normed_ref), channel_id=1, source_target_pairs={{0,2},{1,3},{2,0},{3,1},{4,6},{5,7},{6,4},{7,5},{8,10},{9,11},{10,... | collective-permute-start | bytes 589832 | tf_op jit(solution)/shard_map/ppermute | solution.py:392
  29.1 0.0 collective-permute-done.1.ahead_ref
  29.1 0.0 copy-start.2
  29.1 1.6 %shard_map.103 = (bf16[256,384]{1,0:T(8,128)(2,1)S(1)}, bf16[256,384]{1,0:T(8,128)(2,1)S(1)}) custom-call(s32[16,128]{1,0:T(8,128)S(1)} %get-tuple-element.17.facts_ref, s32[8,128]{1,0:T(8,128)S(1)} %broadcast_in_dim.3.anchor_ref, bf16[16,16,384]{2,1,0:T(8,128)(2,1)S(1)} %get-tuple-element.18.edge_ref.own_ref, ...), custom_call_target="tpu_custom_call" | custom-call | flops 1000000000 | bytes 2585088 | tf_op jit(solution)/shard_map/pallas_call | solution.py:309
  30.7 2.3 %collective-permute-start.4 = (bf16[256,384]{1,0:T(8,128)(2,1)S(1)}, bf16[256,384]{1,0:T(8,128)(2,1)S(1)}, u32[]{:S(2)}, u32[]{:S(2)}) collective-permute-start(bf16[256,384]{1,0:T(8,128)(2,1)S(1)} %get-tuple-element.25.normed_ref), channel_id=1, source_target_pairs={{0,2},{1,3},{2,0},{3,1},{4,6},{5,7},{6,4},{7,5},{8,10},{9,11},{10,... | collective-permute-start | bytes 589832 | tf_op jit(solution)/shard_map/ppermute | solution.py:392
  33.0 0.0 collective-permute-done.3
  33.0 0.0 copy-start
  33.1 0.0 copy-start.1
  33.1 0.0 copy-start.3
  33.1 4.4 %all_gather.6.gathered_ref = bf16[4,256,384]{2,1,0:T(8,128)(2,1)S(1)} all-gather(bf16[2,256,384]{2,1,0:T(8,128)(2,1)S(1)} %pad_maximum_fusion), channel_id=1, replica_groups={{0,1},{2,3},{4,5},{6,7},{8,9},{10,11},{12,13},{14,15},{16,17},{18,19},{..., dimensions={0}, use_global_device_ids=true | all-gather | bytes 1179648 | tf_op jit(solution)/shard_map/all_gather | solution.py:390
  37.5 0.0 copy-done.2
  37.5 0.0 copy-done
  37.5 0.0 copy-done.1
  37.5 0.0 copy-done.3
  37.5 3.1 %shard_map.104._.first_ref = bf16[4,64,384]{2,1,0:T(8,128)(2,1)S(1)} custom-call(s32[16,128]{1,0:T(8,128)S(1)} %get-tuple-element.17.facts_ref, s32[8,128]{1,0:T(8,128)S(1)} %broadcast_in_dim.3.anchor_ref, bf16[256,384]{1,0:T(8,128)(2,1)S(1)} %get-tuple-element.23._.resident_ref, bf16[256,384]{1,0:T(8,128)(2,1)S(1)} %get-tuple-element.26.normed_ref, ...), custom_call_target="tpu_custom_call" | custom-call | flops 1000000000 | bytes 3555840 | tf_op jit(solution)/shard_map/pallas_call | solution.py:309
  40.6 0.5 %shard_map.105.done_ref = bf16[3,256,384]{2,1,0:T(8,128)(2,1)S(1)} custom-call(bf16[256,384]{1,0:T(8,128)(2,1)S(1)} %get-tuple-element.25.normed_ref, bf16[3,384,384]{2,1,0:T(8,128)(2,1)S(1)} %copy-done, bf16[4,64,384]{2,1,0:T(8,128)(2,1)S(1)} %shard_map.104._.first_ref), custom_call_target="tpu_custom_call" | custom-call | flops 1000000000 | bytes 1277952 | tf_op jit(solution)/shard_map/pallas_call | solution.py:309
  41.1 0.0 collective-permute-done.4.swapped_ref
  41.2 2.5 %all_gather.7.gathered_ref = bf16[4,256,384]{2,1,0:T(8,128)(2,1)S(1)} all-gather(bf16[2,256,384]{2,1,0:T(8,128)(2,1)S(1)} %pad_maximum_fusion.1), channel_id=1, replica_groups={{0,1},{2,3},{4,5},{6,7},{8,9},{10,11},{12,13},{14,15},{16,17},{18,19},{..., dimensions={0}, use_global_device_ids=true | all-gather | bytes 1179648 | tf_op jit(solution)/shard_map/all_gather | solution.py:390
  43.7 3.9 %shard_map.106 = bf16[4,2,64,384]{3,2,1,0:T(8,128)(2,1)} custom-call(s32[1]{0:T(128)} %bitcast.core_ref, s32[2]{0:T(128)} %shifts_hbm.3, s32[16,128]{1,0:T(8,128)S(1)} %get-tuple-element.17.facts_ref, s32[8,128]{1,0:T(8,128)S(1)} %broadcast_in_dim.3.anchor_ref, bf16[256,384]{1,0:T(8,128)(2,1)S(1)} %get-tuple-element.24.resident_ref, ...), custom_call_target="tpu_custom_call" | custom-call | flops 1000000000 | bytes 4342280 | tf_op jit(solution)/shard_map/pallas_call | solution.py:309
  (3 shorter events, 0.1 us)
Async XLA Ops:
  0.0 21.7 %copy-start.5 = (bf16[3,384,384]{2,1,0:T(8,128)(2,1)S(1)}, bf16[3,384,384]{2,1,0:T(8,128)(2,1)}, u32[]{:S(2)}) copy-start(bf16[3,384,384]{2,1,0:T(8,128)(2,1)} %qkv_ref.8) | copy-start | bytes 2654212
  1.2 21.7 %collective-permute-start = (bf16[17,16,384]{2,1,0:T(8,128)(2,1)S(1)}, bf16[17,16,384]{2,1,0:T(8,128)(2,1)S(1)}, u32[]{:S(2)}, u32[]{:S(2)}) collective-permute-start(bf16[17,16,384]{2,1,0:T(8,128)(2,1)S(1)} %get-tuple-element.21), channel_id=1, source_target_pairs={{508,0},{0,4},{4,8},{8,12},{12,16},{16,20},{20,24},{24,28},{28,32}... | collective-permute-start | bytes 626696 | tf_op jit(solution)/shard_map/ppermute | solution.py:363
  5.2 16.5 %copy-start.4 = (f32[3,384]{1,0:T(4,128)S(1)}, f32[3,384]{1,0:T(4,128)}, u32[]{:S(2)}) copy-start(f32[3,384]{1,0:T(4,128)} %gains_ref.9) | copy-start | bytes 13828
  5.3 17.6 %collective-permute-start.2 = (bf16[16,16,384]{2,1,0:T(8,128)(2,1)S(1)}, bf16[16,16,384]{2,1,0:T(8,128)(2,1)S(1)}, u32[]{:S(2)}, u32[]{:S(2)}) collective-permute-start(bf16[16,16,384]{2,1,0:T(8,128)(2,1)S(1)} %get-tuple-element.19.other_ref.own_ref), channel_id=1, source_target_pairs={{0,508},{4,0},{8,4},{12,8},{16,12},{20,16},{24,20},{28,24},{32,28}... | collective-permute-start | bytes 589832 | tf_op jit(solution)/shard_map/ppermute | solution.py:364
  18.3 10.8 %collective-permute-start.1 = (bf16[16,16,384]{2,1,0:T(8,128)(2,1)S(1)}, bf16[16,16,384]{2,1,0:T(8,128)(2,1)S(1)}, u32[]{:S(2)}, u32[]{:S(2)}) collective-permute-start(bf16[16,16,384]{2,1,0:T(8,128)(2,1)S(1)} %get-tuple-element.18.edge_ref.own_ref), channel_id=1, source_target_pairs={{0,508},{4,0},{8,4},{12,8},{16,12},{20,16},{24,20},{28,24},{32,28}... | collective-permute-start | bytes 589832 | tf_op jit(solution)/shard_map/ppermute | solution.py:369
  21.7 1.2 %copy-start.6 = (bf16[384,384]{1,0:T(8,128)(2,1)S(1)}, bf16[384,384]{1,0:T(8,128)(2,1)}, u32[]{:S(2)}) copy-start(bf16[384,384]{1,0:T(8,128)(2,1)} %out_w_ref.5) | copy-start | bytes 884740
  24.6 8.4 %collective-permute-start.3 = (bf16[256,384]{1,0:T(8,128)(2,1)S(1)}, bf16[256,384]{1,0:T(8,128)(2,1)S(1)}, u32[]{:S(2)}, u32[]{:S(2)}) collective-permute-start(bf16[256,384]{1,0:T(8,128)(2,1)S(1)} %get-tuple-element.26.normed_ref), channel_id=1, source_target_pairs={{0,2},{1,3},{2,0},{3,1},{4,6},{5,7},{6,4},{7,5},{8,10},{9,11},{10,... | collective-permute-start | bytes 589832 | tf_op jit(solution)/shard_map/ppermute | solution.py:392
  29.1 8.4 %copy-start.2 = (bf16[768,384]{1,0:T(8,128)(2,1)S(1)}, bf16[768,384]{1,0:T(8,128)(2,1)}, u32[]{:S(2)}) copy-start(bf16[768,384]{1,0:T(8,128)(2,1)} %mlp_ref.3) | copy-start | bytes 1769476
  30.7 10.4 %collective-permute-start.4 = (bf16[256,384]{1,0:T(8,128)(2,1)S(1)}, bf16[256,384]{1,0:T(8,128)(2,1)S(1)}, u32[]{:S(2)}, u32[]{:S(2)}) collective-permute-start(bf16[256,384]{1,0:T(8,128)(2,1)S(1)} %get-tuple-element.25.normed_ref), channel_id=1, source_target_pairs={{0,2},{1,3},{2,0},{3,1},{4,6},{5,7},{6,4},{7,5},{8,10},{9,11},{10,... | collective-permute-start | bytes 589832 | tf_op jit(solution)/shard_map/ppermute | solution.py:392
  33.0 4.5 %copy-start = (bf16[3,384,384]{2,1,0:T(8,128)(2,1)S(1)}, bf16[3,384,384]{2,1,0:T(8,128)(2,1)}, u32[]{:S(2)}) copy-start(bf16[3,384,384]{2,1,0:T(8,128)(2,1)} %qkv_ref.11) | copy-start | bytes 2654212
  33.1 4.4 %copy-start.1 = (bf16[384,768]{1,0:T(8,128)(2,1)S(1)}, bf16[384,768]{1,0:T(8,128)(2,1)}, u32[]{:S(2)}) copy-start(bf16[384,768]{1,0:T(8,128)(2,1)} %in_ref.3) | copy-start | bytes 1769476
  33.1 4.4 %copy-start.3 = (bf16[384,384]{1,0:T(8,128)(2,1)S(1)}, bf16[384,384]{1,0:T(8,128)(2,1)}, u32[]{:S(2)}) copy-start(bf16[384,384]{1,0:T(8,128)(2,1)} %out_w_ref.7) | copy-start | bytes 884740
